TPU v7x, 256 devices: a whole 4x4x8 slice. The times are simulated.
256 devices in a mesh: gx: 16 (over y, x), gz: 16 (over z, core).
Axes of the slice: x: 4, y: 4, z: 8, core: 2. Of those that a mesh axis runs over, the one named last changes fastest.
Arguments:
- phase: float32 [4, 256, 256, 512], P(None, 'gx', 'gz'), may hold values from 0 to 1
- solute: float32 [256, 256, 512], P('gx', 'gz'), may hold values from -3 to 3
- grain_map: int32 [4, 256, 256, 512], P(None, 'gx', 'gz'), may hold values from 0 to 1023
- frame_steps: int32 [2], replicated, may hold values from 0 to 15
Outputs:
- phase_out: float32 [4, 256, 256, 512], P(None, 'gx', 'gz')
- solute_out: float32 [256, 256, 512], P('gx', 'gz')
All inputs are finite; a program needn't handle non-finite values.
Results may differ from a plain program's by a relative error of at most 0.0003.
Values sent between devices are 32-bit elements; how exact they have to be, the bound alone decides.
A program may use at most 128 MiB of HBM per device.

v0:
```python
import math

import jax
import jax.numpy as jnp
from jax import lax
from jax.sharding import PartitionSpec as P

ORDERS = 4
STEPS = 2
NGRAIN = 1024


time_step = 0.08
aniso_strength = 0.5
grad_floor = 0.05
well_height = 8.0
intersection_penalty = 2.0
drive_gain = 1.0
solute_diffusion = 1.0
rejection = 0.5
thermal_length = 8.0


def with_halo(cells, sides, width, closed):
    for axis, dim in sides:
        count = lax.axis_size(axis)
        ends = count if closed else count - 1
        head = lax.slice_in_dim(cells, 0, width, axis=dim)
        tail = lax.slice_in_dim(cells, cells.shape[dim] - width, cells.shape[dim], axis=dim)
        cells = jnp.concatenate(
            [
                lax.ppermute(tail, axis, [(i, (i + 1) % count) for i in range(ends)]),
                cells,
                lax.ppermute(head, axis, [((i + 1) % count, i) for i in range(ends)]),
            ],
            axis=dim,
        )
    return cells


def from_behind(block, axis, distance):
    devices = range(lax.axis_size(axis))
    route = [(i - distance, i) for i in devices if i - distance in devices]
    return lax.ppermute(block, axis, route)


def core(ext, grains, offset, zglob, center_plane):
    center = ext[:, 1:-1, 1:-1]
    x_low = ext[:, :-2, 1:-1]
    x_high = ext[:, 2:, 1:-1]
    z_low = ext[:, 1:-1, :-2]
    z_high = ext[:, 1:-1, 2:]
    y_low = jnp.roll(center, 1, axis=3)
    y_high = jnp.roll(center, -1, axis=3)
    lap = x_low + x_high + z_low + z_high + y_low + y_high - 6.0 * center
    phase = center[:ORDERS]
    solute = center[ORDERS]
    grad_x = 0.5 * (x_high[:ORDERS] - x_low[:ORDERS])
    grad_y = 0.5 * (y_high[:ORDERS] - y_low[:ORDERS])
    grad_z = 0.5 * (z_high[:ORDERS] - z_low[:ORDERS])
    angle = grains.astype(jnp.float32) * (2.0 * math.pi / NGRAIN)
    cosine = jnp.cos(angle)
    sine = jnp.sin(angle)
    rot_x = cosine * grad_x + sine * grad_y
    rot_y = cosine * grad_y - sine * grad_x
    squares = grad_x * grad_x + grad_y * grad_y + grad_z * grad_z
    quartic = rot_x**4 + rot_y**4 + grad_z**4
    aniso = 1.0 + aniso_strength * quartic / (squares + grad_floor) ** 2
    intersection = jnp.sum(phase * phase, axis=0)
    well = phase * (1.0 - phase) * (1.0 - 2.0 * phase)
    shape_fn = 30.0 * phase * phase * (1.0 - phase) * (1.0 - phase)
    height = (center_plane - zglob - offset).astype(jnp.float32)
    drive = jnp.tanh(height / thermal_length)[None, :, None] - solute
    delta = time_step * (
        aniso * lap[:ORDERS]
        + well_height * well
        - intersection_penalty * phase * (intersection - phase * phase)
        + drive_gain * shape_fn * drive
    )
    solute_new = (
        solute + time_step * solute_diffusion * lap[ORDERS] + rejection * jnp.sum(delta, axis=0)
    )
    return jnp.concatenate([phase + delta, solute_new[None]], axis=0)


def local(phase, solute, grain_map, frame_steps):
    planes = phase.shape[2]
    base = lax.axis_index("gz") * planes
    zglob = base + jnp.arange(planes, dtype=jnp.int32)
    total_planes = lax.axis_size("gz") * planes
    center_plane = total_planes // 2
    state = jnp.concatenate([phase, solute[None]], axis=0)
    for step in range(STEPS):
        widened = with_halo(state, (("gx", 1),), 1, True)
        tall = with_halo(widened, (("gz", 2),), 1, False)
        state = core(tall, grain_map, frame_steps[step], zglob, center_plane)
    incoming = from_behind(state[:, :, :1], "gz", -1)
    shifted = jnp.concatenate([state[:, :, 1:], incoming], axis=2)
    return (shifted[:ORDERS], shifted[ORDERS])


def solution(mesh):
    in_specs = (P(None, "gx", "gz", None), P("gx", "gz", None), P(None, "gx", "gz", None), P())
    out_specs = (P(None, "gx", "gz", None), P("gx", "gz", None))
    return jax.shard_map(local, mesh=mesh, in_specs=in_specs, out_specs=out_specs, check_vma=False)
```

profile of v0, /device:TPU:97, one launch (start us, length us, event | category | flops | bytes accessed | tf_op | source)
XLA Modules:
  0.0 105.4 jit_solution(16091153552018196122)
XLA Ops:
  0.6 0.0 copy-start
  0.6 0.0 copy-start.2
  0.6 1.1 %fusion.62 = (f32[5,1,16,512]{3,2,1,0:T(8,128)S(1)}, f32[5,1,16,512]{3,2,1,0:T(8,128)S(1)}) fusion(f32[4,16,16,512]{3,2,1,0:T(8,128)} %param.4, f32[1,16,16,512]{3,2,1,0:T(8,128)} %bitcast.23), kind=kLoop, calls=%fused_computation.153 | loop fusion | flops 81920 | bytes 2949120 | tf_op jit(solution)/shard_map/concatenate | solution.py:92
  1.8 1.3 %collective-permute-start.1 = (f32[5,1,16,512]{3,2,1,0:T(8,128)S(1)}, f32[5,1,16,512]{3,2,1,0:T(8,128)S(1)}, u32[]{:S(2)}, u32[]{:S(2)}) collective-permute-start(f32[5,1,16,512]{3,2,1,0:T(8,128)S(1)} %get-tuple-element.25), channel_id=1, source_target_pairs={{0,16},{16,32},{32,48},{48,64},{64,80},{80,96},{96,112},{112,128},... | collective-permute-start | bytes 491528 | tf_op jit(solution)/shard_map/ppermute | solution.py:32
  3.1 3.8 %collective-permute-start = (f32[5,1,16,512]{3,2,1,0:T(8,128)S(1)}, f32[5,1,16,512]{3,2,1,0:T(8,128)S(1)}, u32[]{:S(2)}, u32[]{:S(2)}) collective-permute-start(f32[5,1,16,512]{3,2,1,0:T(8,128)S(1)} %get-tuple-element.26), channel_id=1, source_target_pairs={{16,0},{32,16},{48,32},{64,48},{80,64},{96,80},{112,96},{128,112},... | collective-permute-start | bytes 491528 | tf_op jit(solution)/shard_map/ppermute | solution.py:34
  6.9 0.0 copy-done
  6.9 0.0 copy-done.2
  6.9 0.0 copy-start.11
  6.9 3.2 %fusion.3 = (f32[5,16,16,511]{3,2,1,0:T(8,128)}, f32[5,16,16,511]{3,2,1,0:T(8,128)}) fusion(f32[4,16,16,512]{3,2,1,0:T(8,128)S(1)} %copy-done, f32[1,16,16,512]{3,2,1,0:T(8,128)S(1)} %bitcast.24), kind=kLoop, calls=%fused_computation.47 | loop fusion | flops 1308160 | bytes 7854080 | tf_op jit(solution)/shard_map/concatenate | solution.py:92
  10.1 0.0 copy-done.11
  10.1 0.6 fusion.67
  10.7 1.3 %multiply_tanh_fusion = (f32[16]{0:T(128)S(1)}, f32[16]{0:T(128)S(1)}) fusion(s32[]{:T(128)} %bitcast.4, s32[]{:T(128)S(6)} %mul.250, s32[]{:T(128)} %bitcast.1), kind=kLoop, calls=%fused_computation.155 | loop fusion | flops 128 | bytes 140 | tf_op jit(solution)/shard_map/tanh | solution.py:73
  12.0 0.1 broadcast_subtract_fusion.1
  12.2 0.3 multiply_reduce_fusion.1
  12.4 0.2 fusion.49
  12.7 0.0 collective-permute-done.1
  12.7 0.0 collective-permute-done
  12.7 0.4 pad_maximum_fusion.29
  13.1 5.6 %collective-permute-start.3 = (f32[5,18,1,512]{3,2,1,0:T(1,128)S(1)}, f32[5,18,1,512]{3,2,1,0:T(1,128)S(1)}, u32[]{:S(2)}, u32[]{:S(2)}) collective-permute-start(f32[5,18,1,512]{3,2,1,0:T(1,128)S(1)} %get-tuple-element.11), channel_id=1, source_target_pairs={{0,1},{1,2},{2,3},{3,4},{4,5},{5,6},{6,7},{7,8},{8,9},{9,10},{10,1... | collective-permute-start | bytes 552968 | tf_op jit(solution)/shard_map/ppermute | solution.py:32
  18.7 0.0 copy-start.3
  18.7 0.0 copy-start.4
  18.7 2.3 %collective-permute-start.2 = (f32[5,18,1,512]{3,2,1,0:T(1,128)S(1)}, f32[5,18,1,512]{3,2,1,0:T(1,128)S(1)}, u32[]{:S(2)}, u32[]{:S(2)}) collective-permute-start(f32[5,18,1,512]{3,2,1,0:T(1,128)S(1)} %get-tuple-element.12), channel_id=1, source_target_pairs={{1,0},{2,1},{3,2},{4,3},{5,4},{6,5},{7,6},{8,7},{9,8},{10,9},{11,1... | collective-permute-start | bytes 552968 | tf_op jit(solution)/shard_map/ppermute | solution.py:34
  21.1 0.8 maximum_maximum_fusion
  21.9 0.0 collective-permute-done.3
  21.9 5.2 %collective-permute-done.2 = f32[5,18,1,512]{3,2,1,0:T(1,128)S(1)} collective-permute-done((f32[5,18,1,512]{3,2,1,0:T(1,128)S(1)}, f32[5,18,1,512]{3,2,1,0:T(1,128)S(1)}, u32[]{:S(2)}, u32[]{:S(2)}) %collective-permute-start.2) | collective-permute-done | bytes 184352 | tf_op jit(solution)/shard_map/ppermute | solution.py:34
  27.1 0.0 copy-done.3
  27.1 0.0 copy-done.4
  27.1 0.0 copy-start.8
  27.1 3.8 %fusion.9 = f32[5,16,16,512]{3,2,1,0:T(8,128)S(1)} fusion(f32[5,16,16,1]{3,2,1,0:T(8,128)S(1)} %get-tuple-element.28, f32[5,16,16,1]{3,2,1,0:T(8,128)S(1)} %get-tuple-element.27, f32[1,16,16,512]{3,2,1,0:T(8,128)S(1)} %bitcast.28, f32[4,16,16,512]{3,2,1,0:T(8,128)S(1)} %copy-done, f32[5,18,1,512]{3,2,1,0:T(1,128)S(1)} %collective-permute-done.2, ...), kind=kLoop, calls=%fused_computation.53 | loop fusion | flops 11796480 | bytes 16424960 | tf_op jit(solution)/shard_map/sub | solution.py:55
  30.8 0.0 copy-done.8
  30.9 0.0 copy-start.6
  30.9 17.0 %multiply_reduce_fusion = (f32[16,16,512]{2,1,0:T(8,128)}, f32[4,16,16,512]{3,2,1,0:T(8,128)}, f32[4,16,16,512]{3,2,1,0:T(8,128)}) fusion(f32[4,16,16,512]{3,2,1,0:T(8,128)S(1)} %copy-done, f32[16,16,512]{2,1,0:T(8,128)S(1)} %broadcast_subtract_fusion.1, f32[16,16,512]{2,1,0:T(8,128)S(1)} %multiply_reduce_fusion.1, f32[5,16,16,512]{3,2,1,0:T(8,128)S(1)} %fusion.9, ...), kind=kLoop, calls=%fused_computation.123 | loop fusion | flops 32899072 | bytes 22716416 | tf_op jit(solution)/shard_map/reduce_sum | solution.py:69
  47.9 0.0 copy-done.6
  47.9 2.8 %reduce_sum.37 = f32[16,16,512]{2,1,0:T(8,128)} reduce(f32[4,16,16,512]{3,2,1,0:T(8,128)} %get-tuple-element.6, f32[]{:T(128)} %constant.7.clone.1), dimensions={0}, to_apply=%region_1.2 | reduce | flops 393216 | bytes 2621444 | tf_op jit(solution)/shard_map/reduce_sum | solution.py:81
  50.7 1.4 %broadcast_subtract_fusion = (f32[16,16,512]{2,1,0:T(8,128)S(1)}, f32[16,16,512]{2,1,0:T(8,128)S(1)}) fusion(f32[16]{0:T(128)S(1)} %get-tuple-element.31, f32[16,16,512]{2,1,0:T(8,128)} %reduce_sum.37, f32[16,16,512]{2,1,0:T(8,128)S(1)} %copy-done.2, f32[5,16,16,512]{3,2,1,0:T(8,128)} %copy-done.6), kind=kLoop, calls=%fused_computation.140 | loop fusion | flops 655360 | bytes 2621504 | tf_op jit(solution)/shard_map/sub | solution.py:73
  52.1 0.0 copy-done.1
  52.1 0.1 collective-permute-start.5
  52.2 4.8 %collective-permute-start.4 = (f32[5,1,16,512]{3,2,1,0:T(8,128)S(1)}, f32[5,1,16,512]{3,2,1,0:T(8,128)S(1)}, u32[]{:S(2)}, u32[]{:S(2)}) collective-permute-start(f32[5,1,16,512]{3,2,1,0:T(8,128)S(1)} %get-tuple-element.18), channel_id=1, source_target_pairs={{16,0},{32,16},{48,32},{64,48},{80,64},{96,80},{112,96},{128,112},... | collective-permute-start | bytes 491528 | tf_op jit(solution)/shard_map/ppermute | solution.py:34
  57.0 1.0 fusion.1
  58.0 0.2 fusion.47
  58.3 1.4 %collective-permute-done.5 = f32[5,1,16,512]{3,2,1,0:T(8,128)S(1)} collective-permute-done((f32[5,1,16,512]{3,2,1,0:T(8,128)S(1)}, f32[5,1,16,512]{3,2,1,0:T(8,128)S(1)}, u32[]{:S(2)}, u32[]{:S(2)}) %collective-permute-start.5) | collective-permute-done | bytes 163872 | tf_op jit(solution)/shard_map/ppermute | solution.py:32
  59.7 0.0 collective-permute-done.4
  59.7 0.4 pad_maximum_fusion.25
  60.1 3.8 %collective-permute-start.7 = (f32[5,18,1,512]{3,2,1,0:T(1,128)S(1)}, f32[5,18,1,512]{3,2,1,0:T(1,128)S(1)}, u32[]{:S(2)}, u32[]{:S(2)}) collective-permute-start(f32[5,18,1,512]{3,2,1,0:T(1,128)S(1)} %get-tuple-element.9), channel_id=1, source_target_pairs={{0,1},{1,2},{2,3},{3,4},{4,5},{5,6},{6,7},{7,8},{8,9},{9,10},{10,1... | collective-permute-start | bytes 552968 | tf_op jit(solution)/shard_map/ppermute | solution.py:32
  63.8 2.1 %collective-permute-start.6 = (f32[5,18,1,512]{3,2,1,0:T(1,128)S(1)}, f32[5,18,1,512]{3,2,1,0:T(1,128)S(1)}, u32[]{:S(2)}, u32[]{:S(2)}) collective-permute-start(f32[5,18,1,512]{3,2,1,0:T(1,128)S(1)} %get-tuple-element.10), channel_id=1, source_target_pairs={{1,0},{2,1},{3,2},{4,3},{5,4},{6,5},{7,6},{8,7},{9,8},{10,9},{11,1... | collective-permute-start | bytes 552968 | tf_op jit(solution)/shard_map/ppermute | solution.py:34
  65.9 0.8 maximum_maximum_fusion.1
  66.7 0.0 collective-permute-done.7
  66.8 5.1 %collective-permute-done.6 = f32[5,18,1,512]{3,2,1,0:T(1,128)S(1)} collective-permute-done((f32[5,18,1,512]{3,2,1,0:T(1,128)S(1)}, f32[5,18,1,512]{3,2,1,0:T(1,128)S(1)}, u32[]{:S(2)}, u32[]{:S(2)}) %collective-permute-start.6) | collective-permute-done | bytes 184352 | tf_op jit(solution)/shard_map/ppermute | solution.py:34
  71.9 3.7 %fusion.6 = f32[5,16,16,512]{3,2,1,0:T(8,128)S(1)} fusion(f32[5,16,16,1]{3,2,1,0:T(8,128)S(1)} %get-tuple-element.20, f32[5,16,16,1]{3,2,1,0:T(8,128)S(1)} %get-tuple-element.19, f32[1,16,16,512]{3,2,1,0:T(8,128)S(1)} %bitcast.35, f32[4,16,16,512]{3,2,1,0:T(8,128)S(1)} %copy-done.1, f32[5,18,1,512]{3,2,1,0:T(1,128)S(1)} %collective-permute-done.6, ...), kind=kLoop, calls=%fused_computation.50 | loop fusion | flops 11796480 | bytes 16424960 | tf_op jit(solution)/shard_map/sub | solution.py:55
  75.7 0.0 copy-start.7
  75.7 0.0 copy-done.9
  75.7 0.0 copy-done.10
  75.7 16.0 %fusion.63 = (f32[4,16,16,512]{3,2,1,0:T(8,128)}, f32[4,16,16,512]{3,2,1,0:T(8,128)}) fusion(f32[4,16,16,512]{3,2,1,0:T(8,128)S(1)} %copy-done.1, f32[16,16,512]{2,1,0:T(8,128)S(1)} %get-tuple-element.7, f32[16,16,512]{2,1,0:T(8,128)S(1)} %copy-done.10, f32[5,16,16,512]{3,2,1,0:T(8,128)S(1)} %fusion.6, f32[5,1,16,512]{3,2,1,0:T(8,128)S(1)} %collective-permute-done.4, ...), kind=kLoop, calls=%fused_computation.158 | loop fusion | flops 31981568 | bytes 22192128 | tf_op jit(solution)/shard_map/add | solution.py:83
  91.7 0.0 copy-done.7
  91.7 0.0 copy-start.5
  91.7 2.0 %reduce_sum.39 = f32[16,16,512]{2,1,0:T(8,128)S(1)} reduce(f32[4,16,16,512]{3,2,1,0:T(8,128)} %get-tuple-element.3, f32[]{:T(128)} %constant.7.clone.1), dimensions={0}, to_apply=%region_3.4 | reduce | flops 393216 | bytes 2621444 | tf_op jit(solution)/shard_map/reduce_sum | solution.py:81
  93.8 1.2 %fusion.55 = f32[1,16,16,512]{3,2,1,0:T(8,128)S(1)} fusion(f32[16,16,512]{2,1,0:T(8,128)S(1)} %get-tuple-element.8, f32[5,16,16,512]{3,2,1,0:T(8,128)} %copy-done.7, f32[16,16,512]{2,1,0:T(8,128)S(1)} %reduce_sum.39), kind=kLoop, calls=%fused_computation.135 | loop fusion | flops 524288 | bytes 2097152 | tf_op jit(solution)/shard_map/broadcast_in_dim | solution.py:83
  95.0 0.0 copy-done.5
  95.0 0.1 pad_maximum_fusion.33
  95.1 1.9 %collective-permute-start.8 = (f32[5,16,1,512]{3,2,1,0:T(1,128)S(1)}, f32[5,16,1,512]{3,2,1,0:T(1,128)S(1)}, u32[]{:S(2)}, u32[]{:S(2)}) collective-permute-start(f32[5,16,1,512]{3,2,1,0:T(1,128)S(1)} %pad_maximum_fusion.33), channel_id=1, source_target_pairs={{1,0},{2,1},{3,2},{4,3},{5,4},{6,5},{7,6},{8,7},{9,8},{10,9},{11,1... | collective-permute-start | bytes 491528 | tf_op jit(solution)/shard_map/ppermute | solution.py:44
  97.0 0.5 slice_maximum_fusion
  97.5 5.5 %collective-permute-done.8 = f32[5,16,1,512]{3,2,1,0:T(1,128)S(1)} collective-permute-done((f32[5,16,1,512]{3,2,1,0:T(1,128)S(1)}, f32[5,16,1,512]{3,2,1,0:T(1,128)S(1)}, u32[]{:S(2)}, u32[]{:S(2)}) %collective-permute-start.8) | collective-permute-done | bytes 163872 | tf_op jit(solution)/shard_map/ppermute | solution.py:44
  102.9 0.9 fusion.51
  103.8 1.6 %fusion.24 = f32[4,16,16,512]{3,2,1,0:T(8,128)} fusion(f32[5,16,15,512]{3,2,1,0:T(8,128)S(1)} %slice_maximum_fusion, f32[5,16,1,512]{3,2,1,0:T(1,128)S(1)} %collective-permute-done.8), kind=kLoop, calls=%fused_computation.93 | loop fusion | flops 524288 | bytes 4718592 | tf_op jit(solution)/shard_map/concatenate | solution.py:98
  (4 shorter events, 0.0 us)
Async XLA Ops:
  0.6 6.3 %copy-start = (f32[4,16,16,512]{3,2,1,0:T(8,128)S(1)}, f32[4,16,16,512]{3,2,1,0:T(8,128)}, u32[]{:S(2)}) copy-start(f32[4,16,16,512]{3,2,1,0:T(8,128)} %param.4) | copy-start | bytes 6291460
  0.6 6.3 %copy-start.2 = (f32[16,16,512]{2,1,0:T(8,128)S(1)}, f32[16,16,512]{2,1,0:T(8,128)}, u32[]{:S(2)}) copy-start(f32[16,16,512]{2,1,0:T(8,128)} %param.5) | copy-start | bytes 1572868
  1.8 10.9 %collective-permute-start.1 = (f32[5,1,16,512]{3,2,1,0:T(8,128)S(1)}, f32[5,1,16,512]{3,2,1,0:T(8,128)S(1)}, u32[]{:S(2)}, u32[]{:S(2)}) collective-permute-start(f32[5,1,16,512]{3,2,1,0:T(8,128)S(1)} %get-tuple-element.25), channel_id=1, source_target_pairs={{0,16},{16,32},{32,48},{48,64},{64,80},{80,96},{96,112},{112,128},... | collective-permute-start | bytes 491528 | tf_op jit(solution)/shard_map/ppermute | solution.py:32
  3.1 9.6 %collective-permute-start = (f32[5,1,16,512]{3,2,1,0:T(8,128)S(1)}, f32[5,1,16,512]{3,2,1,0:T(8,128)S(1)}, u32[]{:S(2)}, u32[]{:S(2)}) collective-permute-start(f32[5,1,16,512]{3,2,1,0:T(8,128)S(1)} %get-tuple-element.26), channel_id=1, source_target_pairs={{16,0},{32,16},{48,32},{64,48},{80,64},{96,80},{112,96},{128,112},... | collective-permute-start | bytes 491528 | tf_op jit(solution)/shard_map/ppermute | solution.py:34
  6.9 3.2 %copy-start.11 = (s32[2]{0:T(128)S(1)}, s32[2]{0:T(128)}, u32[]{:S(2)}) copy-start(s32[2]{0:T(128)} %param.7) | copy-start | bytes 28
  13.1 8.8 %collective-permute-start.3 = (f32[5,18,1,512]{3,2,1,0:T(1,128)S(1)}, f32[5,18,1,512]{3,2,1,0:T(1,128)S(1)}, u32[]{:S(2)}, u32[]{:S(2)}) collective-permute-start(f32[5,18,1,512]{3,2,1,0:T(1,128)S(1)} %get-tuple-element.11), channel_id=1, source_target_pairs={{0,1},{1,2},{2,3},{3,4},{4,5},{5,6},{6,7},{7,8},{8,9},{9,10},{10,1... | collective-permute-start | bytes 552968 | tf_op jit(solution)/shard_map/ppermute | solution.py:32
  18.7 8.4 %copy-start.3 = (f32[5,16,16,511]{3,2,1,0:T(8,128)S(1)}, f32[5,16,16,511]{3,2,1,0:T(8,128)}, u32[]{:S(2)}) copy-start(f32[5,16,16,511]{3,2,1,0:T(8,128)} %get-tuple-element.21) | copy-start | bytes 7848964
  18.7 8.3 %copy-start.4 = (f32[5,16,16,511]{3,2,1,0:T(8,128)S(1)}, f32[5,16,16,511]{3,2,1,0:T(8,128)}, u32[]{:S(2)}) copy-start(f32[5,16,16,511]{3,2,1,0:T(8,128)} %get-tuple-element.22) | copy-start | bytes 7848964
  18.7 8.3 %collective-permute-start.2 = (f32[5,18,1,512]{3,2,1,0:T(1,128)S(1)}, f32[5,18,1,512]{3,2,1,0:T(1,128)S(1)}, u32[]{:S(2)}, u32[]{:S(2)}) collective-permute-start(f32[5,18,1,512]{3,2,1,0:T(1,128)S(1)} %get-tuple-element.12), channel_id=1, source_target_pairs={{1,0},{2,1},{3,2},{4,3},{5,4},{6,5},{7,6},{8,7},{9,8},{10,9},{11,1... | collective-permute-start | bytes 552968 | tf_op jit(solution)/shard_map/ppermute | solution.py:34
  27.1 3.8 %copy-start.8 = (s32[4,16,16,512]{3,2,1,0:T(8,128)S(1)}, s32[4,16,16,512]{3,2,1,0:T(8,128)}, u32[]{:S(2)}) copy-start(s32[4,16,16,512]{3,2,1,0:T(8,128)} %param.6) | copy-start | bytes 6291460
  30.9 17.0 %copy-start.6 = (f32[5,16,16,512]{3,2,1,0:T(8,128)}, f32[5,16,16,512]{3,2,1,0:T(8,128)S(1)}, u32[]{:S(2)}) copy-start(f32[5,16,16,512]{3,2,1,0:T(8,128)S(1)} %fusion.9) | copy-start | bytes 7864324
  47.9 4.2 %copy-start.1 = (f32[4,16,16,512]{3,2,1,0:T(8,128)S(1)}, f32[4,16,16,512]{3,2,1,0:T(8,128)}, u32[]{:S(2)}) copy-start(f32[4,16,16,512]{3,2,1,0:T(8,128)} %get-tuple-element.5) | copy-start | bytes 6291460
  52.1 7.6 %collective-permute-start.5 = (f32[5,1,16,512]{3,2,1,0:T(8,128)S(1)}, f32[5,1,16,512]{3,2,1,0:T(8,128)S(1)}, u32[]{:S(2)}, u32[]{:S(2)}) collective-permute-start(f32[5,1,16,512]{3,2,1,0:T(8,128)S(1)} %get-tuple-element.17), channel_id=1, source_target_pairs={{0,16},{16,32},{32,48},{48,64},{64,80},{80,96},{96,112},{112,128},... | collective-permute-start | bytes 491528 | tf_op jit(solution)/shard_map/ppermute | solution.py:32
  52.2 7.5 %collective-permute-start.4 = (f32[5,1,16,512]{3,2,1,0:T(8,128)S(1)}, f32[5,1,16,512]{3,2,1,0:T(8,128)S(1)}, u32[]{:S(2)}, u32[]{:S(2)}) collective-permute-start(f32[5,1,16,512]{3,2,1,0:T(8,128)S(1)} %get-tuple-element.18), channel_id=1, source_target_pairs={{16,0},{32,16},{48,32},{64,48},{80,64},{96,80},{112,96},{128,112},... | collective-permute-start | bytes 491528 | tf_op jit(solution)/shard_map/ppermute | solution.py:34
  60.1 6.7 %collective-permute-start.7 = (f32[5,18,1,512]{3,2,1,0:T(1,128)S(1)}, f32[5,18,1,512]{3,2,1,0:T(1,128)S(1)}, u32[]{:S(2)}, u32[]{:S(2)}) collective-permute-start(f32[5,18,1,512]{3,2,1,0:T(1,128)S(1)} %get-tuple-element.9), channel_id=1, source_target_pairs={{0,1},{1,2},{2,3},{3,4},{4,5},{5,6},{6,7},{7,8},{8,9},{9,10},{10,1... | collective-permute-start | bytes 552968 | tf_op jit(solution)/shard_map/ppermute | solution.py:32
  63.8 8.1 %collective-permute-start.6 = (f32[5,18,1,512]{3,2,1,0:T(1,128)S(1)}, f32[5,18,1,512]{3,2,1,0:T(1,128)S(1)}, u32[]{:S(2)}, u32[]{:S(2)}) collective-permute-start(f32[5,18,1,512]{3,2,1,0:T(1,128)S(1)} %get-tuple-element.10), channel_id=1, source_target_pairs={{1,0},{2,1},{3,2},{4,3},{5,4},{6,5},{7,6},{8,7},{9,8},{10,9},{11,1... | collective-permute-start | bytes 552968 | tf_op jit(solution)/shard_map/ppermute | solution.py:34
  71.9 3.8 %copy-start.9 = (s32[4,16,16,512]{3,2,1,0:T(8,128)S(1)}, s32[4,16,16,512]{3,2,1,0:T(8,128)}, u32[]{:S(2)}) copy-start(s32[4,16,16,512]{3,2,1,0:T(8,128)} %param.6) | copy-start | bytes 6291460
  71.9 3.8 %copy-start.10 = (f32[16,16,512]{2,1,0:T(8,128)S(1)}, f32[16,16,512]{2,1,0:T(8,128)}, u32[]{:S(2)}) copy-start(f32[16,16,512]{2,1,0:T(8,128)} %get-tuple-element.4) | copy-start | bytes 1572868
  75.7 16.1 %copy-start.7 = (f32[5,16,16,512]{3,2,1,0:T(8,128)}, f32[5,16,16,512]{3,2,1,0:T(8,128)S(1)}, u32[]{:S(2)}) copy-start(f32[5,16,16,512]{3,2,1,0:T(8,128)S(1)} %fusion.6) | copy-start | bytes 7864324
  91.7 3.2 %copy-start.5 = (f32[4,16,16,512]{3,2,1,0:T(8,128)S(1)}, f32[4,16,16,512]{3,2,1,0:T(8,128)}, u32[]{:S(2)}) copy-start(f32[4,16,16,512]{3,2,1,0:T(8,128)} %get-tuple-element.2) | copy-start | bytes 6291460
  95.1 7.8 %collective-permute-start.8 = (f32[5,16,1,512]{3,2,1,0:T(1,128)S(1)}, f32[5,16,1,512]{3,2,1,0:T(1,128)S(1)}, u32[]{:S(2)}, u32[]{:S(2)}) collective-permute-start(f32[5,16,1,512]{3,2,1,0:T(1,128)S(1)} %pad_maximum_fusion.33), channel_id=1, source_target_pairs={{1,0},{2,1},{3,2},{4,3},{5,4},{6,5},{7,6},{8,7},{9,8},{10,9},{11,1... | collective-permute-start | bytes 491528 | tf_op jit(solution)/shard_map/ppermute | solution.py:44
where the time goes:
time: 106 us; the launch traced here: 105 us
  other arithmetic  60.8 us (57%)
  starting transfers between devices  25.7 us (24%)
  waiting for transfers between devices  17.2 us (16%)
    reduce_sum x2, other arithmetic, core(): intersection = jnp.sum(phase * phase, axis=0)  17.3 us
    add x1, other arithmetic, core(): return jnp.concatenate([phase + delta, solute_new[None]], axis=0)  16 us
    ppermute x4, starting transfers between devices, with_halo(): lax.ppermute(head, axis, [((i + 1) % count, i) for i in range(ends)])  13 us
    ppermute x4, starting transfers between devices, with_halo(): lax.ppermute(tail, axis, [(i, (i + 1) % count) for i in range(ends)])  10.8 us
    ppermute x4, waiting for transfers between devices, with_halo(): lax.ppermute(head, axis, [((i + 1) % count, i) for i in range(ends)])  10.3 us
    sub x2, other arithmetic, core(): lap = x_low + x_high + z_low + z_high + y_low + y_high - 6.0 * center  7.5 us
    ppermute x1, waiting for transfers between devices, from_behind(): return lax.ppermute(block, axis, route)  5.46 us
    reduce_sum x2, other arithmetic, core(): jnp.sum(delta, axis=0)  4.82 us
  transfers between devices with their start and end apart: 9, of which 4 were waited for; matrix products, arithmetic and copies ran while one was open for 9% of the time, Pallas kernels for 0%

commit v1 on v0

v1 whole, which is shorter than its diff:
```python
import math

import jax
import jax.numpy as jnp
import numpy as np
from jax import lax
from jax.experimental import pallas as pl
from jax.experimental.pallas import tpu as pltpu
from jax.sharding import PartitionSpec as P

ORDERS = 4
FIELDS = 5
STEPS = 2
NGRAIN = 1024
NZ = 256
CX = 16
CZ = 16
NY = 512
LANES = 128
YT = NY // LANES
GROUP = 4
GROUPS = CX // GROUP
MESH = pl.DeviceIdType.MESH

BASE0 = 8


def sine_coefficients():
    nodes = np.cos(np.pi * (np.arange(400) + 0.5) / 400)
    theta = nodes * np.pi / 2
    even = np.polynomial.chebyshev.Chebyshev.fit(nodes, np.cos(theta), 8, domain=[-1, 1])
    odd = np.polynomial.chebyshev.Chebyshev.fit(nodes, np.sin(theta), 9, domain=[-1, 1])
    even = even.convert(kind=np.polynomial.Polynomial).coef
    odd = odd.convert(kind=np.polynomial.Polynomial).coef
    cos_c = [float(even[i] * math.sqrt(0.5) / 128.0**i) for i in (0, 2, 4, 6, 8)]
    sin_c = [float(odd[i] * math.sqrt(2.0) / 128.0**i) for i in (1, 3, 5, 7, 9)]
    return sin_c, cos_c


SIN_C, COS_C = sine_coefficients()


def horner(x, coefficients):
    value = coefficients[-1]
    for c in coefficients[-2::-1]:
        value = value * x + c
    return value


def next_y(rolled, offset):
    if offset > 0:
        return jnp.concatenate([rolled[1:], rolled[:1]], axis=0)
    return jnp.concatenate([rolled[-1:], rolled[:-1]], axis=0)


def neighbours(s, f, xi, row):
    at = pl.ds(row, 8)
    c = s[f, xi, :, at, :]
    xl = s[f, xi - 1, :, at, :]
    xh = s[f, xi + 1, :, at, :]
    zl = s[f, xi, :, pl.ds(row - 1, 8), :]
    zh = s[f, xi, :, pl.ds(row + 1, 8), :]
    lane = lax.broadcasted_iota(jnp.int32, c.shape, 2)
    right = pltpu.roll(c, 1, axis=2)
    left = pltpu.roll(c, LANES - 1, axis=2)
    yl = jnp.where(lane == 0, next_y(right, -1), right)
    yh = jnp.where(lane == LANES - 1, next_y(left, 1), left)
    return c, xl, xh, yl, yh, zl, zh


def advance(s, cs, x, row, cs_row, thermal, put):
    xi = x + 1
    u = s[ORDERS, xi, :, pl.ds(row, 8), :]
    drive = thermal - 2.4 * u
    q = None
    for k in range(ORDERS):
        p = s[k, xi, :, pl.ds(row, 8), :]
        q = p * p if q is None else q + p * p
    well = 0.64 - 0.16 * q
    total = None
    for k in range(ORDERS):
        p, xl, xh, yl, yh, zl, zh = neighbours(s, k, xi, row)
        gx, gy, gz = xh - xl, yh - yl, zh - zl
        lap = (xl + xh) + (yl + yh) + (zl + zh) - 6.0 * p
        x2, y2, z2 = gx * gx, gy * gy, gz * gz
        r = x2 + y2
        at = pl.ds(cs_row, 8)
        t = cs[0, k, x, :, at, :] * (gx * gy) + cs[1, k, x, :, at, :] * (x2 - y2)
        quartic = r * r + z2 * z2 - t * t
        d = (r + z2) + 0.2
        ratio = quartic * pl.reciprocal(d * d, approx=True)
        w = p - p * p
        delta = (
            lap * (0.08 + 0.04 * ratio)
            + p * (well + p * (1.44 * p - 1.92))
            + (w * w) * drive
        )
        put(k, p + delta)
        total = delta if total is None else total + delta
    c, xl, xh, yl, yh, zl, zh = neighbours(s, ORDERS, xi, row)
    near = (xl + xh) + (yl + yh) + (zl + zh)
    put(ORDERS, 0.52 * c + 0.08 * near + 0.5 * total)


def kernel(
    frames, phase, solute, grain, phase_out, solute_out,
    s0, s1, g, cs, o,
    load_sem, out_sem, x_send, x_recv, z_send, z_recv, m_send, m_recv, c_send, c_recv, d_send, d_recv,
):
    gx, gz = lax.axis_index("gx"), lax.axis_index("gz")
    n_gx, n_gz = lax.axis_size("gx"), lax.axis_size("gz")
    right, left = lax.rem(gx + 1, n_gx), lax.rem(gx + n_gx - 1, n_gx)
    has_up, has_down = gz < n_gz - 1, gz > 0

    loads = []
    for k in range(YT):
        lanes = pl.ds(k * LANES, LANES)
        rows = pl.ds(BASE0, CZ)
        loads.append(
            (
                pltpu.make_async_copy(
                    phase.at[:, :, :, lanes], s0.at[pl.ds(0, ORDERS), pl.ds(1, CX), k, rows, :], load_sem.at[0, k]
                ),
                pltpu.make_async_copy(
                    solute.at[:, :, lanes], s0.at[ORDERS, pl.ds(1, CX), k, rows, :], load_sem.at[1, k]
                ),
                pltpu.make_async_copy(grain.at[:, :, :, lanes], g.at[:, :, k, :, :], load_sem.at[2, k]),
            )
        )
    for which in range(3):
        for k in range(YT):
            loads[k][which].start()

    barrier = pltpu.get_barrier_semaphore()

    def greet(ix, iz):
        pl.semaphore_signal(barrier, inc=1, device_id=(ix, iz), device_id_type=MESH)

    greet(left, gz)
    greet(right, gz)

    @pl.when(has_up)
    def _():
        greet(gx, gz + 1)
        greet(left, gz + 1)
        greet(right, gz + 1)

    @pl.when(has_down)
    def _():
        greet(gx, gz - 1)
        greet(left, gz - 1)
        greet(right, gz - 1)

    @pl.when(jnp.logical_not(has_down))
    def _():
        s0[:, :, :, pl.ds(BASE0 - 1, 1), :] = jnp.zeros((FIELDS, CX + 2, YT, 1, LANES), jnp.float32)

    @pl.when(jnp.logical_not(has_up))
    def _():
        s0[:, :, :, pl.ds(BASE0 + CZ, 1), :] = jnp.zeros((FIELDS, CX + 2, YT, 1, LANES), jnp.float32)
        s1[:, :, :, pl.ds(CZ, 2), :] = jnp.zeros((FIELDS, CX + 2, YT, 2, LANES), jnp.float32)
        cs[:, :, :, :, pl.ds(CZ, 1), :] = jnp.zeros((2, ORDERS, CX, YT, 1, LANES), jnp.float32)

    def remote(src, dst, send, recv, ix, iz):
        return pltpu.make_async_remote_copy(
            src_ref=src, dst_ref=dst, send_sem=send, recv_sem=recv, device_id=(ix, iz), device_id_type=MESH
        )

    def x_copy(step, way):
        s, rows = (s0, pl.ds(BASE0, CZ)) if step == 0 else (s1, pl.ds(0, CZ))
        src, dst, to = (CX, 0, right) if way == 0 else (1, CX + 1, left)
        return remote(
            s.at[:, src, :, rows, :], s.at[:, dst, :, rows, :], x_send.at[step, way], x_recv.at[step, way], to, gz
        )

    def z_copy(group, way):
        planes = pl.ds(1 + group * GROUP, GROUP)
        src, dst, to = (BASE0 + CZ - 1, BASE0 - 1, gz + 1) if way == 0 else (BASE0, BASE0 + CZ, gz - 1)
        return remote(
            s0.at[:, planes, :, pl.ds(src, 1), :],
            s0.at[:, planes, :, pl.ds(dst, 1), :],
            z_send.at[way, group],
            z_recv.at[way, group],
            gx,
            to,
        )

    def m_copy(group):
        planes = pl.ds(1 + group * GROUP, GROUP)
        return remote(
            s1.at[:, planes, :, pl.ds(0, 2), :],
            s1.at[:, planes, :, pl.ds(CZ, 2), :],
            m_send.at[group],
            m_recv.at[group],
            gx,
            gz - 1,
        )

    def d_copy(way):
        src, dst, to = (CX, 0, right) if way == 0 else (1, CX + 1, left)
        return remote(
            s1.at[:, src, :, pl.ds(0, 1), :],
            s1.at[:, dst, :, pl.ds(CZ, 1), :],
            d_send.at[way],
            d_recv.at[way],
            to,
            gz - 1,
        )

    def c_copy():
        return remote(
            cs.at[:, :, :, :, pl.ds(0, 1), :], cs.at[:, :, :, :, pl.ds(CZ, 1), :], c_send, c_recv, gx, gz - 1
        )

    for which in range(2):
        for k in range(YT):
            loads[k][which].wait()

    pl.semaphore_wait(barrier, 2 + 3 * (has_up.astype(jnp.int32) + has_down.astype(jnp.int32)))

    x_copy(0, 0).start()
    x_copy(0, 1).start()
    order = (1, 2, 3, 0)
    for group in order:

        @pl.when(has_up)
        def _(group=group):
            z_copy(group, 0).start()

        @pl.when(has_down)
        def _(group=group):
            z_copy(group, 1).start()

    for k in range(YT):
        loads[k][2].wait()

    def trig(x, carry):
        for k in range(ORDERS):
            for half in range(2):
                at = pl.ds(8 * half, 8)
                h = ((g[k, x, :, at, :] & 255) - 128).astype(jnp.float32)
                h2 = h * h
                cs[0, k, x, :, at, :] = h * horner(h2, SIN_C)
                cs[1, k, x, :, at, :] = horner(h2, COS_C)
        return carry

    lax.fori_loop(0, CX, trig, 0)

    @pl.when(has_down)
    def _():
        c_copy().start()

    def thermal(step, first):
        z = gz * CZ + first + lax.broadcasted_iota(jnp.int32, (1, 8, LANES), 1)
        height = (NZ // 2 - z - frames[step]).astype(jnp.float32)
        return 2.4 * jnp.tanh(height * 0.125)

    heat = [thermal(0, 0), thermal(0, 8)]

    def first_step(i, carry):
        x = lax.rem(i + GROUP, CX)

        @pl.when(lax.rem(i, GROUP) == 0)
        def _():
            group = lax.div(x, GROUP)

            @pl.when(has_down)
            def _():
                z_copy(group, 0).wait_recv()

            @pl.when(has_up)
            def _():
                z_copy(group, 1).wait_recv()

        @pl.when(x == CX - 1)
        def _():
            x_copy(0, 1).wait_recv()

        @pl.when(x == 0)
        def _():
            x_copy(0, 0).wait_recv()

        for half in range(2):

            def put(f, value, half=half):
                s1[f, x + 1, :, pl.ds(8 * half, 8), :] = value

            advance(s0, cs, x, BASE0 + 8 * half, 8 * half, heat[half], put)

        @pl.when(x == CX - 1)
        def _():
            x_copy(1, 0).start()

            @pl.when(has_down)
            def _():
                d_copy(0).start()

        @pl.when(x == 0)
        def _():
            x_copy(1, 1).start()

            @pl.when(has_down)
            def _():
                d_copy(1).start()

        @pl.when(jnp.logical_and(lax.rem(i, GROUP) == GROUP - 1, has_down))
        def _():
            m_copy(lax.div(x, GROUP)).start()

        return carry

    lax.fori_loop(0, CX, first_step, 0)

    @pl.when(has_up)
    def _():
        c_copy().wait_recv()
        for group in range(GROUPS):
            m_copy(group).wait_recv()

    heat2 = [thermal(1, 1), thermal(1, 9)]

    def out_copies(x):
        return (
            pltpu.make_async_copy(o.at[pl.ds(0, ORDERS), x], phase_out.at[:, x], out_sem.at[0, x]),
            pltpu.make_async_copy(o.at[ORDERS, x], solute_out.at[x], out_sem.at[1, x]),
        )

    def second_step(i, carry):
        x = lax.rem(i + 1, CX)

        @pl.when(x == CX - 1)
        def _():
            x_copy(1, 1).wait_recv()

            @pl.when(has_up)
            def _():
                d_copy(1).wait_recv()

        @pl.when(x == 0)
        def _():
            x_copy(1, 0).wait_recv()

            @pl.when(has_up)
            def _():
                d_copy(0).wait_recv()

        for half in range(2):

            def put(f, value, half=half):
                for k in range(YT):
                    o[f, x, pl.ds(8 * half, 8), pl.ds(k * LANES, LANES)] = value[k]

            advance(s1, cs, x, 1 + 8 * half, 1 + 8 * half, heat2[half], put)

        @pl.when(jnp.logical_not(has_up))
        def _():
            o[:, x, pl.ds(CZ - 1, 1), :] = jnp.zeros((FIELDS, 1, NY), jnp.float32)

        for copy in out_copies(x):
            copy.start()
        return carry

    lax.fori_loop(0, CX, second_step, 0)

    def finish(x, carry):
        for copy in out_copies(x):
            copy.wait()
        return carry

    lax.fori_loop(0, CX, finish, 0)
    for step in range(STEPS):
        for way in range(2):
            x_copy(step, way).wait_send()

    @pl.when(has_up)
    def _():
        for group in range(GROUPS):
            z_copy(group, 0).wait_send()

    @pl.when(has_down)
    def _():
        for group in range(GROUPS):
            z_copy(group, 1).wait_send()
            m_copy(group).wait_send()
        c_copy().wait_send()
        d_copy(0).wait_send()
        d_copy(1).wait_send()


def local(phase, solute, grain_map, frame_steps):
    anywhere = pl.BlockSpec(memory_space=pl.ANY)
    dma = pltpu.SemaphoreType.DMA
    return pl.pallas_call(
        kernel,
        out_shape=(
            jax.ShapeDtypeStruct(phase.shape, jnp.float32),
            jax.ShapeDtypeStruct(solute.shape, jnp.float32),
        ),
        in_specs=[pl.BlockSpec(memory_space=pltpu.SMEM), anywhere, anywhere, anywhere],
        out_specs=(anywhere, anywhere),
        scratch_shapes=[
            pltpu.VMEM((FIELDS, CX + 2, YT, 32, LANES), jnp.float32),
            pltpu.VMEM((FIELDS, CX + 2, YT, 24, LANES), jnp.float32),
            pltpu.VMEM((ORDERS, CX, YT, CZ, LANES), jnp.int32),
            pltpu.VMEM((2, ORDERS, CX, YT, 24, LANES), jnp.float32),
            pltpu.VMEM((FIELDS, CX, CZ, NY), jnp.float32),
            dma((3, YT)),
            dma((2, CX)),
            dma((STEPS, 2)),
            dma((STEPS, 2)),
            dma((2, GROUPS)),
            dma((2, GROUPS)),
            dma((GROUPS,)),
            dma((GROUPS,)),
            dma,
            dma,
            dma((2,)),
            dma((2,)),
        ],
        compiler_params=pltpu.CompilerParams(
            collective_id=0, has_side_effects=True, vmem_limit_bytes=48 * 1024 * 1024
        ),
        name="grow",
    )(frame_steps, phase, solute, grain_map)


def solution(mesh):
    in_specs = (P(None, "gx", "gz", None), P("gx", "gz", None), P(None, "gx", "gz", None), P())
    out_specs = (P(None, "gx", "gz", None), P("gx", "gz", None))
    return jax.shard_map(local, mesh=mesh, in_specs=in_specs, out_specs=out_specs, check_vma=False)
```

time: 106 us -> 33.2 us (0.31)
  other arithmetic: 60.8 us -> 0 us
  Pallas kernels: 0 us -> 27 us
  starting transfers between devices: 25.7 us -> 0 us
  waiting for transfers between devices: 17.2 us -> 0 us
  local copies, waits for them, and re-layouts: 0.63 us -> 5.39 us
    pallas_call x0 -> x1, Pallas kernels: none -> 27 us  [local(): pl.pallas_call(kernel, out_shape=(jax.ShapeDtypeStruct(phase.shape, jnp.f...]
    ppermute x9 -> x0, starting transfers between devices: 25.7 us -> none  [the longest x4 13 us: with_halo(): lax.ppermute(head, axis, [((i + 1) % count, i) for i in range(ends)])]
    reduce_sum x4 -> x0, other arithmetic: 22.1 us -> none  [the longest x2 17.3 us: core(): intersection = jnp.sum(phase * phase, axis=0)]
    ppermute x9 -> x0, waiting for transfers between devices: 17.2 us -> none  [the longest x4 10.3 us: with_halo(): lax.ppermute(head, axis, [((i + 1) % count, i) for i in range(ends)])]
    add x1 -> x0, other arithmetic: 16 us -> none  [core(): return jnp.concatenate([phase + delta, solute_new[None]], axis=0)]
    concatenate x13 -> x0, other arithmetic: 10.3 us -> none  [the longest x3 4.61 us: local(): state = jnp.concatenate([phase, solute[None]], axis=0)]
    sub x4 -> x0, other arithmetic: 9.03 us -> none  [the longest x2 7.5 us: core(): lap = x_low + x_high + z_low + z_high + y_low + y_high - 6.0 * center]
    unnamed x24 -> x8, local copies, waits for them, and re-layouts: 0.05 us -> 5.39 us
  transfers between devices with their start and end apart: 9 -> 0, of which waited for: 4 -> 0; matrix products, arithmetic and copies ran while one was open for 9% -> 0% of each run, Pallas kernels for 0% -> 0%
where the time goes in v1:
time: 33.2 us; the launch traced here: 33 us
  Pallas kernels  27 us (81%)
  local copies, waits for them, and re-layouts  5.39 us (16%)
  between operations  0.65 us (2%)
    pallas_call x1, Pallas kernels, local(): pl.pallas_call(kernel, out_shape=(jax.ShapeDtypeStruct(phase.shape, jnp.f...  27 us
    unnamed x8, local copies, waits for them, and re-layouts  5.39 us

profile of v1, /device:TPU:97, one launch (start us, length us, event | category | flops | bytes accessed | tf_op | source)
XLA Modules:
  0.0 33.0 jit_solution(15927904558258629316)
XLA Ops:
  0.6 0.0 copy-start
  0.6 1.6 %copy-done = f32[4,16,16,512]{3,2,1,0:T(8,128)S(1)} copy-done((f32[4,16,16,512]{3,2,1,0:T(8,128)S(1)}, f32[4,16,16,512]{3,2,1,0:T(8,128)}, u32[]{:S(2)}) %copy-start) | copy-done | bytes 2097176
  2.2 0.0 copy-start.1
  2.2 1.0 %copy-done.1 = f32[16,16,512]{2,1,0:T(8,128)S(1)} copy-done((f32[16,16,512]{2,1,0:T(8,128)S(1)}, f32[16,16,512]{2,1,0:T(8,128)}, u32[]{:S(2)}) %copy-start.1) | copy-done | bytes 524312
  3.3 0.0 copy-start.2
  3.3 0.7 %copy-done.2 = s32[2]{0:T(128)S(1)} copy-done((s32[2]{0:T(128)S(1)}, s32[2]{0:T(128)}, u32[]{:S(2)}) %copy-start.2) | copy-done | bytes 32
  3.9 27.0 %grow.1 = (f32[4,16,16,512]{3,2,1,0:T(8,128)S(1)}, f32[16,16,512]{2,1,0:T(8,128)S(1)}) custom-call(s32[2]{0:T(128)S(1)} %copy-done.2, f32[4,16,16,512]{3,2,1,0:T(8,128)S(1)} %copy-done, f32[16,16,512]{2,1,0:T(8,128)S(1)} %copy-done.1, s32[4,16,16,512]{3,2,1,0:T(8,128)} %grain.1), custom_call_target="tpu_custom_call" | custom-call | tf_op jit(solution)/shard_map/grow/pallas_call | solution.py:393
  30.9 1.3 %copy.8 = f32[4,16,16,512]{3,2,1,0:T(8,128)} copy(f32[4,16,16,512]{3,2,1,0:T(8,128)S(1)} %get-tuple-element.4) | data formatting | bytes 4194304
  32.2 0.8 %copy.9 = f32[16,16,512]{2,1,0:T(8,128)} copy(f32[16,16,512]{2,1,0:T(8,128)S(1)} %get-tuple-element.5) | data formatting | bytes 1048576
Async XLA Ops:
  0.6 1.6 %copy-start = (f32[4,16,16,512]{3,2,1,0:T(8,128)S(1)}, f32[4,16,16,512]{3,2,1,0:T(8,128)}, u32[]{:S(2)}) copy-start(f32[4,16,16,512]{3,2,1,0:T(8,128)} %phase.1) | copy-start | bytes 6291460
  2.2 1.0 %copy-start.1 = (f32[16,16,512]{2,1,0:T(8,128)S(1)}, f32[16,16,512]{2,1,0:T(8,128)}, u32[]{:S(2)}) copy-start(f32[16,16,512]{2,1,0:T(8,128)} %solute.1) | copy-start | bytes 1572868
  3.3 0.7 %copy-start.2 = (s32[2]{0:T(128)S(1)}, s32[2]{0:T(128)}, u32[]{:S(2)}) copy-start(s32[2]{0:T(128)} %frames.1) | copy-start | bytes 28

commit v2 on v1

--- a/solution.py
+++ b/solution.py
@@ -104,7 +104,7 @@
 
 def kernel(
     frames, phase, solute, grain, phase_out, solute_out,
-    s0, s1, g, cs, o,
+    s0, s1, g, cs, o, heat,
     load_sem, out_sem, x_send, x_recv, z_send, z_recv, m_send, m_recv, c_send, c_recv, d_send, d_recv,
 ):
     gx, gz = lax.axis_index("gx"), lax.axis_index("gz")
@@ -127,50 +127,65 @@
                 pltpu.make_async_copy(grain.at[:, :, :, lanes], g.at[:, :, k, :, :], load_sem.at[2, k]),
             )
         )
+    barrier = pltpu.get_barrier_semaphore()
+
+    def greet(ix, iz):
+        pl.semaphore_signal(barrier, inc=1, device_id=(ix, iz), device_id_type=MESH)
+
+    greet(left, gz)
+    greet(right, gz)
+
+    @pl.when(has_up)
+    def _():
+        greet(gx, gz + 1)
+
+    @pl.when(has_down)
+    def _():
+        greet(gx, gz - 1)
+
     for which in range(3):
         for k in range(YT):
             loads[k][which].start()
 
-    barrier = pltpu.get_barrier_semaphore()
-
-    def greet(ix, iz):
-        pl.semaphore_signal(barrier, inc=1, device_id=(ix, iz), device_id_type=MESH)
-
-    greet(left, gz)
-    greet(right, gz)
-
-    @pl.when(has_up)
-    def _():
-        greet(gx, gz + 1)
-        greet(left, gz + 1)
-        greet(right, gz + 1)
-
-    @pl.when(has_down)
-    def _():
-        greet(gx, gz - 1)
-        greet(left, gz - 1)
-        greet(right, gz - 1)
-
     @pl.when(jnp.logical_not(has_down))
     def _():
-        s0[:, :, :, pl.ds(BASE0 - 1, 1), :] = jnp.zeros((FIELDS, CX + 2, YT, 1, LANES), jnp.float32)
+        def clear(x, carry):
+            s0[:, x, :, pl.ds(BASE0 - 1, 1), :] = jnp.zeros((FIELDS, YT, 1, LANES), jnp.float32)
+            return carry
+
+        lax.fori_loop(0, CX + 2, clear, 0)
 
     @pl.when(jnp.logical_not(has_up))
     def _():
-        s0[:, :, :, pl.ds(BASE0 + CZ, 1), :] = jnp.zeros((FIELDS, CX + 2, YT, 1, LANES), jnp.float32)
-        s1[:, :, :, pl.ds(CZ, 2), :] = jnp.zeros((FIELDS, CX + 2, YT, 2, LANES), jnp.float32)
-        cs[:, :, :, :, pl.ds(CZ, 1), :] = jnp.zeros((2, ORDERS, CX, YT, 1, LANES), jnp.float32)
+        def clear(x, carry):
+            s0[:, x, :, pl.ds(BASE0 + CZ, 1), :] = jnp.zeros((FIELDS, YT, 1, LANES), jnp.float32)
+            s1[:, x, :, pl.ds(CZ, 2), :] = jnp.zeros((FIELDS, YT, 2, LANES), jnp.float32)
+            return carry
+
+        lax.fori_loop(0, CX + 2, clear, 0)
+
+        def clear_cs(x, carry):
+            cs[:, :, x, :, pl.ds(CZ, 1), :] = jnp.zeros((2, ORDERS, YT, 1, LANES), jnp.float32)
+            return carry
+
+        lax.fori_loop(0, CX, clear_cs, 0)
 
     def remote(src, dst, send, recv, ix, iz):
         return pltpu.make_async_remote_copy(
             src_ref=src, dst_ref=dst, send_sem=send, recv_sem=recv, device_id=(ix, iz), device_id_type=MESH
         )
 
-    def x_copy(step, way):
-        s, rows = (s0, pl.ds(BASE0, CZ)) if step == 0 else (s1, pl.ds(0, CZ))
+    def x_copy(step, way, half):
+        s, base = (s0, BASE0) if step == 0 else (s1, 0)
+        rows = pl.ds(base + 8 * half, 8)
         src, dst, to = (CX, 0, right) if way == 0 else (1, CX + 1, left)
         return remote(
-            s.at[:, src, :, rows, :], s.at[:, dst, :, rows, :], x_send.at[step, way], x_recv.at[step, way], to, gz
+            s.at[:, src, :, rows, :],
+            s.at[:, dst, :, rows, :],
+            x_send.at[step, way, half],
+            x_recv.at[step, way, half],
+            to,
+            gz,
         )
 
     def z_copy(group, way):
@@ -185,13 +200,12 @@
             to,
         )
 
-    def m_copy(group):
-        planes = pl.ds(1 + group * GROUP, GROUP)
+    def m_copy(x):
         return remote(
-            s1.at[:, planes, :, pl.ds(0, 2), :],
-            s1.at[:, planes, :, pl.ds(CZ, 2), :],
-            m_send.at[group],
-            m_recv.at[group],
+            s1.at[:, x + 1, :, pl.ds(0, 2), :],
+            s1.at[:, x + 1, :, pl.ds(CZ, 2), :],
+            m_send.at[x],
+            m_recv.at[x],
             gx,
             gz - 1,
         )
@@ -216,12 +230,12 @@
         for k in range(YT):
             loads[k][which].wait()
 
-    pl.semaphore_wait(barrier, 2 + 3 * (has_up.astype(jnp.int32) + has_down.astype(jnp.int32)))
-
-    x_copy(0, 0).start()
-    x_copy(0, 1).start()
-    order = (1, 2, 3, 0)
-    for group in order:
+    pl.semaphore_wait(barrier, 2 + has_up.astype(jnp.int32) + has_down.astype(jnp.int32))
+
+    for half in range(2):
+        x_copy(0, 0, half).start()
+        x_copy(0, 1, half).start()
+    for group in (1, 2, 3, 0):
 
         @pl.when(has_up)
         def _(group=group):
@@ -250,19 +264,20 @@
     def _():
         c_copy().start()
 
-    def thermal(step, first):
-        z = gz * CZ + first + lax.broadcasted_iota(jnp.int32, (1, 8, LANES), 1)
-        height = (NZ // 2 - z - frames[step]).astype(jnp.float32)
-        return 2.4 * jnp.tanh(height * 0.125)
-
-    heat = [thermal(0, 0), thermal(0, 8)]
+    for step in range(STEPS):
+        for half in range(2):
+            z = gz * CZ + 8 * half + step + lax.broadcasted_iota(jnp.int32, (1, 8, LANES), 1)
+            height = (NZ // 2 - z - frames[step]).astype(jnp.float32)
+            heat[step, half] = 2.4 * jnp.tanh(height * 0.125)
 
     def first_step(i, carry):
-        x = lax.rem(i + GROUP, CX)
-
-        @pl.when(lax.rem(i, GROUP) == 0)
-        def _():
-            group = lax.div(x, GROUP)
+        m, half = lax.div(i, 2), lax.rem(i, 2)
+        xa = jnp.where(m < 5, 4 + 2 * m, jnp.where(m == 5, 2, 21 - m))
+        xb = jnp.where(m < 6, xa + 1, m - 6)
+
+        @pl.when(jnp.logical_or(i == 0, jnp.logical_or(i == 4, jnp.logical_or(i == 8, i == 10))))
+        def _():
+            group = lax.div(xa, GROUP)
 
             @pl.when(has_down)
             def _():
@@ -272,105 +287,110 @@
             def _():
                 z_copy(group, 1).wait_recv()
 
-        @pl.when(x == CX - 1)
-        def _():
-            x_copy(0, 1).wait_recv()
-
-        @pl.when(x == 0)
-        def _():
-            x_copy(0, 0).wait_recv()
-
-        for half in range(2):
-
-            def put(f, value, half=half):
+        @pl.when(m == 6)
+        def _():
+            x_copy(0, 0, half).wait_recv()
+            x_copy(0, 1, half).wait_recv()
+
+        for x in (xa, xb):
+
+            def put(f, value, x=x):
                 s1[f, x + 1, :, pl.ds(8 * half, 8), :] = value
 
-            advance(s0, cs, x, BASE0 + 8 * half, 8 * half, heat[half], put)
-
-        @pl.when(x == CX - 1)
-        def _():
-            x_copy(1, 0).start()
-
-            @pl.when(has_down)
+            advance(s0, cs, x, BASE0 + 8 * half, 8 * half, heat[0, half], put)
+
+        @pl.when(m == 6)
+        def _():
+            x_copy(1, 0, half).start()
+            x_copy(1, 1, half).start()
+
+        @pl.when(jnp.logical_and(half == 0, has_down))
+        def _():
+            m_copy(xa).start()
+            m_copy(xb).start()
+
+            @pl.when(m == 6)
             def _():
                 d_copy(0).start()
-
-        @pl.when(x == 0)
-        def _():
-            x_copy(1, 1).start()
-
-            @pl.when(has_down)
-            def _():
                 d_copy(1).start()
 
-        @pl.when(jnp.logical_and(lax.rem(i, GROUP) == GROUP - 1, has_down))
-        def _():
-            m_copy(lax.div(x, GROUP)).start()
-
         return carry
 
     lax.fori_loop(0, CX, first_step, 0)
 
-    @pl.when(has_up)
-    def _():
-        c_copy().wait_recv()
-        for group in range(GROUPS):
-            m_copy(group).wait_recv()
-
-    heat2 = [thermal(1, 1), thermal(1, 9)]
-
-    def out_copies(x):
+    def out_copies(x, half):
+        rows = pl.ds(8 * half, 8)
         return (
-            pltpu.make_async_copy(o.at[pl.ds(0, ORDERS), x], phase_out.at[:, x], out_sem.at[0, x]),
-            pltpu.make_async_copy(o.at[ORDERS, x], solute_out.at[x], out_sem.at[1, x]),
+            pltpu.make_async_copy(o.at[pl.ds(0, ORDERS), x, rows, :], phase_out.at[:, x, rows, :], out_sem.at[0, x, half]),
+            pltpu.make_async_copy(o.at[ORDERS, x, rows, :], solute_out.at[x, rows, :], out_sem.at[1, x, half]),
         )
 
     def second_step(i, carry):
-        x = lax.rem(i + 1, CX)
-
-        @pl.when(x == CX - 1)
-        def _():
-            x_copy(1, 1).wait_recv()
-
-            @pl.when(has_up)
-            def _():
-                d_copy(1).wait_recv()
-
-        @pl.when(x == 0)
-        def _():
-            x_copy(1, 0).wait_recv()
-
-            @pl.when(has_up)
-            def _():
-                d_copy(0).wait_recv()
-
+        rim = i >= 14
+        half = jnp.where(rim, i - 14, lax.div(i, 7))
+        m = lax.rem(i, 7)
+        xa = jnp.where(rim, 0, jnp.where(m < 5, 5 + 2 * m, 13 - 2 * m))
+        xb = jnp.where(rim, CX - 1, xa + 1)
+
+        @pl.when(jnp.logical_and(has_up, i == 7))
+        def _():
+            c_copy().wait_recv()
+            m_copy(4).wait_recv()
+            m_copy(5).wait_recv()
+
+        @pl.when(jnp.logical_and(has_up, jnp.logical_and(i >= 7, i < 14)))
+        def _():
+            first = jnp.where(m < 5, xa + 1, xa - 1)
+            m_copy(first).wait_recv()
+            m_copy(first + 1).wait_recv()
+
+        @pl.when(i == 14)
+        def _():
+            for part in range(2):
+                x_copy(1, 0, part).wait_recv()
+                x_copy(1, 1, part).wait_recv()
+
+        @pl.when(jnp.logical_and(i == 15, has_up))
+        def _():
+            d_copy(0).wait_recv()
+            d_copy(1).wait_recv()
+
+        for x in (xa, xb):
+
+            def put(f, value, x=x):
+                for k in range(YT):
+                    o[f, x, pl.ds(pl.multiple_of(8 * half, 8), 8), pl.ds(k * LANES, LANES)] = value[k]
+
+            advance(s1, cs, x, 1 + 8 * half, 1 + 8 * half, heat[1, half], put)
+
+        @pl.when(jnp.logical_and(half == 1, jnp.logical_not(has_up)))
+        def _():
+            for x in (xa, xb):
+                o[:, x, pl.ds(CZ - 1, 1), :] = jnp.zeros((FIELDS, 1, NY), jnp.float32)
+
+        for x in (xa, xb):
+            for copy in out_copies(x, half):
+                copy.start()
+        return carry
+
+    lax.fori_loop(0, CX, second_step, 0)
+
+    def finish(x, carry):
         for half in range(2):
-
-            def put(f, value, half=half):
-                for k in range(YT):
-                    o[f, x, pl.ds(8 * half, 8), pl.ds(k * LANES, LANES)] = value[k]
-
-            advance(s1, cs, x, 1 + 8 * half, 1 + 8 * half, heat2[half], put)
-
-        @pl.when(jnp.logical_not(has_up))
-        def _():
-            o[:, x, pl.ds(CZ - 1, 1), :] = jnp.zeros((FIELDS, 1, NY), jnp.float32)
-
-        for copy in out_copies(x):
-            copy.start()
-        return carry
-
-    lax.fori_loop(0, CX, second_step, 0)
-
-    def finish(x, carry):
-        for copy in out_copies(x):
-            copy.wait()
+            for copy in out_copies(x, half):
+                copy.wait()
+
+        @pl.when(has_down)
+        def _():
+            m_copy(x).wait_send()
+
         return carry
 
     lax.fori_loop(0, CX, finish, 0)
     for step in range(STEPS):
         for way in range(2):
-            x_copy(step, way).wait_send()
+            for half in range(2):
+                x_copy(step, way, half).wait_send()
 
     @pl.when(has_up)
     def _():
@@ -381,14 +401,13 @@
     def _():
         for group in range(GROUPS):
             z_copy(group, 1).wait_send()
-            m_copy(group).wait_send()
         c_copy().wait_send()
         d_copy(0).wait_send()
         d_copy(1).wait_send()
 
 
 def local(phase, solute, grain_map, frame_steps):
-    anywhere = pl.BlockSpec(memory_space=pl.ANY)
+    hbm = pl.BlockSpec(memory_space=pltpu.HBM)
     dma = pltpu.SemaphoreType.DMA
     return pl.pallas_call(
         kernel,
@@ -396,22 +415,23 @@
             jax.ShapeDtypeStruct(phase.shape, jnp.float32),
             jax.ShapeDtypeStruct(solute.shape, jnp.float32),
         ),
-        in_specs=[pl.BlockSpec(memory_space=pltpu.SMEM), anywhere, anywhere, anywhere],
-        out_specs=(anywhere, anywhere),
+        in_specs=[pl.BlockSpec(memory_space=pltpu.SMEM), hbm, hbm, hbm],
+        out_specs=(hbm, hbm),
         scratch_shapes=[
             pltpu.VMEM((FIELDS, CX + 2, YT, 32, LANES), jnp.float32),
             pltpu.VMEM((FIELDS, CX + 2, YT, 24, LANES), jnp.float32),
             pltpu.VMEM((ORDERS, CX, YT, CZ, LANES), jnp.int32),
             pltpu.VMEM((2, ORDERS, CX, YT, 24, LANES), jnp.float32),
             pltpu.VMEM((FIELDS, CX, CZ, NY), jnp.float32),
+            pltpu.VMEM((STEPS, 2, 1, 8, LANES), jnp.float32),
             dma((3, YT)),
-            dma((2, CX)),
-            dma((STEPS, 2)),
-            dma((STEPS, 2)),
+            dma((2, CX, 2)),
+            dma((STEPS, 2, 2)),
+            dma((STEPS, 2, 2)),
             dma((2, GROUPS)),
             dma((2, GROUPS)),
-            dma((GROUPS,)),
-            dma((GROUPS,)),
+            dma((CX,)),
+            dma((CX,)),
             dma,
             dma,
             dma((2,)),

time: 33.2 us -> 29.9 us (0.901)
  Pallas kernels: 27 us -> 23.7 us
    pallas_call x1, Pallas kernels: 27 us -> 23.7 us  [local(): pl.pallas_call(kernel, out_shape=(jax.ShapeDtypeStruct(phase.shape, jnp.f...]
where the time goes in v2:
time: 29.9 us; the launch traced here: 29.7 us
  Pallas kernels  23.7 us (79%)
  local copies, waits for them, and re-layouts  5.39 us (18%)
  between operations  0.65 us (2%)
    pallas_call x1, Pallas kernels, local(): pl.pallas_call(kernel, out_shape=(jax.ShapeDtypeStruct(phase.shape, jnp.f...  23.7 us
    unnamed x8, local copies, waits for them, and re-layouts  5.39 us

profile of v2, /device:TPU:97, one launch (start us, length us, event | category | flops | bytes accessed | tf_op | source)
XLA Modules:
  0.0 29.7 jit_solution(4150401976971913456)
XLA Ops:
  0.6 0.0 copy-start
  0.6 1.6 %copy-done = f32[4,16,16,512]{3,2,1,0:T(8,128)S(1)} copy-done((f32[4,16,16,512]{3,2,1,0:T(8,128)S(1)}, f32[4,16,16,512]{3,2,1,0:T(8,128)}, u32[]{:S(2)}) %copy-start) | copy-done | bytes 2097176
  2.2 0.0 copy-start.1
  2.2 1.0 %copy-done.1 = f32[16,16,512]{2,1,0:T(8,128)S(1)} copy-done((f32[16,16,512]{2,1,0:T(8,128)S(1)}, f32[16,16,512]{2,1,0:T(8,128)}, u32[]{:S(2)}) %copy-start.1) | copy-done | bytes 524312
  3.3 0.0 copy-start.2
  3.3 0.7 %copy-done.2 = s32[2]{0:T(128)S(1)} copy-done((s32[2]{0:T(128)S(1)}, s32[2]{0:T(128)}, u32[]{:S(2)}) %copy-start.2) | copy-done | bytes 32
  3.9 23.7 %grow.1 = (f32[4,16,16,512]{3,2,1,0:T(8,128)S(1)}, f32[16,16,512]{2,1,0:T(8,128)S(1)}) custom-call(s32[2]{0:T(128)S(1)} %copy-done.2, f32[4,16,16,512]{3,2,1,0:T(8,128)S(1)} %copy-done, f32[16,16,512]{2,1,0:T(8,128)S(1)} %copy-done.1, s32[4,16,16,512]{3,2,1,0:T(8,128)} %grain.1), custom_call_target="tpu_custom_call" | custom-call | tf_op jit(solution)/shard_map/grow/pallas_call | solution.py:412
  27.6 1.3 %copy.8 = f32[4,16,16,512]{3,2,1,0:T(8,128)} copy(f32[4,16,16,512]{3,2,1,0:T(8,128)S(1)} %get-tuple-element.4) | data formatting | bytes 4194304
  28.9 0.8 %copy.9 = f32[16,16,512]{2,1,0:T(8,128)} copy(f32[16,16,512]{2,1,0:T(8,128)S(1)} %get-tuple-element.5) | data formatting | bytes 1048576
Async XLA Ops:
  0.6 1.6 %copy-start = (f32[4,16,16,512]{3,2,1,0:T(8,128)S(1)}, f32[4,16,16,512]{3,2,1,0:T(8,128)}, u32[]{:S(2)}) copy-start(f32[4,16,16,512]{3,2,1,0:T(8,128)} %phase.1) | copy-start | bytes 6291460
  2.2 1.0 %copy-start.1 = (f32[16,16,512]{2,1,0:T(8,128)S(1)}, f32[16,16,512]{2,1,0:T(8,128)}, u32[]{:S(2)}) copy-start(f32[16,16,512]{2,1,0:T(8,128)} %solute.1) | copy-start | bytes 1572868
  3.3 0.7 %copy-start.2 = (s32[2]{0:T(128)S(1)}, s32[2]{0:T(128)}, u32[]{:S(2)}) copy-start(s32[2]{0:T(128)} %frames.1) | copy-start | bytes 28

commit v3 on v2

--- a/solution.py
+++ b/solution.py
@@ -103,9 +103,9 @@
 
 
 def kernel(
-    frames, phase, solute, grain, phase_out, solute_out,
-    s0, s1, g, cs, o, heat,
-    load_sem, out_sem, x_send, x_recv, z_send, z_recv, m_send, m_recv, c_send, c_recv, d_send, d_recv,
+    frames_in, phase, solute, grain, o,
+    s0, s1, g, cs, heat, frames,
+    load_sem, frame_sem, x_send, x_recv, z_send, z_recv, m_send, m_recv, c_send, c_recv, d_send, d_recv,
 ):
     gx, gz = lax.axis_index("gx"), lax.axis_index("gz")
     n_gx, n_gz = lax.axis_size("gx"), lax.axis_size("gz")
@@ -127,6 +127,7 @@
                 pltpu.make_async_copy(grain.at[:, :, :, lanes], g.at[:, :, k, :, :], load_sem.at[2, k]),
             )
         )
+    frame_load = pltpu.make_async_copy(frames_in, frames, frame_sem)
     barrier = pltpu.get_barrier_semaphore()
 
     def greet(ix, iz):
@@ -146,6 +147,8 @@
     for which in range(3):
         for k in range(YT):
             loads[k][which].start()
+
+    frame_load.start()
 
     @pl.when(jnp.logical_not(has_down))
     def _():
@@ -264,6 +267,7 @@
     def _():
         c_copy().start()
 
+    frame_load.wait()
     for step in range(STEPS):
         for half in range(2):
             z = gz * CZ + 8 * half + step + lax.broadcasted_iota(jnp.int32, (1, 8, LANES), 1)
@@ -317,13 +321,6 @@
         return carry
 
     lax.fori_loop(0, CX, first_step, 0)
-
-    def out_copies(x, half):
-        rows = pl.ds(8 * half, 8)
-        return (
-            pltpu.make_async_copy(o.at[pl.ds(0, ORDERS), x, rows, :], phase_out.at[:, x, rows, :], out_sem.at[0, x, half]),
-            pltpu.make_async_copy(o.at[ORDERS, x, rows, :], solute_out.at[x, rows, :], out_sem.at[1, x, half]),
-        )
 
     def second_step(i, carry):
         rim = i >= 14
@@ -368,25 +365,10 @@
             for x in (xa, xb):
                 o[:, x, pl.ds(CZ - 1, 1), :] = jnp.zeros((FIELDS, 1, NY), jnp.float32)
 
-        for x in (xa, xb):
-            for copy in out_copies(x, half):
-                copy.start()
         return carry
 
     lax.fori_loop(0, CX, second_step, 0)
 
-    def finish(x, carry):
-        for half in range(2):
-            for copy in out_copies(x, half):
-                copy.wait()
-
-        @pl.when(has_down)
-        def _():
-            m_copy(x).wait_send()
-
-        return carry
-
-    lax.fori_loop(0, CX, finish, 0)
     for step in range(STEPS):
         for way in range(2):
             for half in range(2):
@@ -401,31 +383,42 @@
     def _():
         for group in range(GROUPS):
             z_copy(group, 1).wait_send()
+        for x in range(CX):
+            m_copy(x).wait_send()
         c_copy().wait_send()
         d_copy(0).wait_send()
         d_copy(1).wait_send()
 
 
+def flush(o, phase_out, solute_out, sem):
+    copies = (
+        pltpu.make_async_copy(o.at[pl.ds(0, ORDERS)], phase_out, sem.at[0]),
+        pltpu.make_async_copy(o.at[ORDERS], solute_out, sem.at[1]),
+    )
+    for copy in copies:
+        copy.start()
+    for copy in copies:
+        copy.wait()
+
+
 def local(phase, solute, grain_map, frame_steps):
-    hbm = pl.BlockSpec(memory_space=pltpu.HBM)
+    hbm, vmem = pl.BlockSpec(memory_space=pltpu.HBM), pl.BlockSpec(memory_space=pltpu.VMEM)
     dma = pltpu.SemaphoreType.DMA
-    return pl.pallas_call(
+    args = [pltpu.with_memory_space_constraint(a, pltpu.HBM) for a in (frame_steps, phase, solute, grain_map)]
+    result = pl.pallas_call(
         kernel,
-        out_shape=(
-            jax.ShapeDtypeStruct(phase.shape, jnp.float32),
-            jax.ShapeDtypeStruct(solute.shape, jnp.float32),
-        ),
-        in_specs=[pl.BlockSpec(memory_space=pltpu.SMEM), hbm, hbm, hbm],
-        out_specs=(hbm, hbm),
+        out_shape=pltpu.VMEM((FIELDS, CX, CZ, NY), jnp.float32),
+        in_specs=[hbm] * 4,
+        out_specs=vmem,
         scratch_shapes=[
             pltpu.VMEM((FIELDS, CX + 2, YT, 32, LANES), jnp.float32),
             pltpu.VMEM((FIELDS, CX + 2, YT, 24, LANES), jnp.float32),
             pltpu.VMEM((ORDERS, CX, YT, CZ, LANES), jnp.int32),
             pltpu.VMEM((2, ORDERS, CX, YT, 24, LANES), jnp.float32),
-            pltpu.VMEM((FIELDS, CX, CZ, NY), jnp.float32),
             pltpu.VMEM((STEPS, 2, 1, 8, LANES), jnp.float32),
+            pltpu.SMEM((STEPS,), jnp.int32),
             dma((3, YT)),
-            dma((2, CX, 2)),
+            dma,
             dma((STEPS, 2, 2)),
             dma((STEPS, 2, 2)),
             dma((2, GROUPS)),
@@ -438,10 +431,22 @@
             dma((2,)),
         ],
         compiler_params=pltpu.CompilerParams(
-            collective_id=0, has_side_effects=True, vmem_limit_bytes=48 * 1024 * 1024
+            collective_id=0, has_side_effects=True, vmem_limit_bytes=32 * 1024 * 1024
         ),
         name="grow",
-    )(frame_steps, phase, solute, grain_map)
+    )(*args)
+    return pl.pallas_call(
+        flush,
+        out_shape=(
+            pltpu.HBM(phase.shape, jnp.float32),
+            pltpu.HBM(solute.shape, jnp.float32),
+        ),
+        in_specs=[vmem],
+        out_specs=(hbm, hbm),
+        scratch_shapes=[dma((2,))],
+        compiler_params=pltpu.CompilerParams(vmem_limit_bytes=4 * 1024 * 1024),
+        name="flush",
+    )(result)
 
 
 def solution(mesh):

time: 29.9 us -> 23.7 us (0.79)
  local copies, waits for them, and re-layouts: 5.39 us -> 0 us
  Pallas kernels: 23.7 us -> 22.8 us
    unnamed x8 -> x0, local copies, waits for them, and re-layouts: 5.39 us -> none
    pallas_call x1 -> x2, Pallas kernels: 23.7 us -> 22.8 us  [the longest x1 21.3 us: local(): pl.pallas_call(kernel, out_shape=pltpu.VMEM((FIELDS, CX, CZ, NY), jnp.flo...]
where the time goes in v3:
time: 23.7 us; the launch traced here: 23.5 us
  Pallas kernels  22.8 us (96%)
  between operations  0.64 us (3%)
    pallas_call x1, Pallas kernels, local(): pl.pallas_call(kernel, out_shape=pltpu.VMEM((FIELDS, CX, CZ, NY), jnp.flo...  21.3 us
    pallas_call x1, Pallas kernels, local(): pl.pallas_call(flush, out_shape=(pltpu.HBM(phase.shape, jnp.float32), plt...  1.5 us

profile of v3, /device:TPU:97, one launch (start us, length us, event | category | flops | bytes accessed | tf_op | source)
XLA Modules:
  0.0 23.5 jit_solution(15512323135157338620)
XLA Ops:
  0.6 21.3 %grow.1.o = f32[5,16,16,512]{3,2,1,0:T(8,128)S(1)} custom-call(s32[2]{0:T(128)} %frames_in.1, f32[4,16,16,512]{3,2,1,0:T(8,128)} %phase.1, f32[16,16,512]{2,1,0:T(8,128)} %solute.1, s32[4,16,16,512]{3,2,1,0:T(8,128)} %grain.1), custom_call_target="tpu_custom_call" | custom-call | tf_op jit(solution)/shard_map/grow/pallas_call | solution.py:408
  22.0 1.5 %flush.1 = (f32[4,16,16,512]{3,2,1,0:T(8,128)}, f32[16,16,512]{2,1,0:T(8,128)}) custom-call(f32[5,16,16,512]{3,2,1,0:T(8,128)S(1)} %grow.1.o), custom_call_target="tpu_custom_call" | custom-call | tf_op jit(solution)/shard_map/flush/pallas_call | solution.py:438

commit v4 on v3

--- a/solution.py
+++ b/solution.py
@@ -274,100 +274,109 @@
             height = (NZ // 2 - z - frames[step]).astype(jnp.float32)
             heat[step, half] = 2.4 * jnp.tanh(height * 0.125)
 
-    def first_step(i, carry):
-        m, half = lax.div(i, 2), lax.rem(i, 2)
-        xa = jnp.where(m < 5, 4 + 2 * m, jnp.where(m == 5, 2, 21 - m))
-        xb = jnp.where(m < 6, xa + 1, m - 6)
-
-        @pl.when(jnp.logical_or(i == 0, jnp.logical_or(i == 4, jnp.logical_or(i == 8, i == 10))))
-        def _():
-            group = lax.div(xa, GROUP)
-
-            @pl.when(has_down)
-            def _():
-                z_copy(group, 0).wait_recv()
+    def first_units(planes, halves):
+        for x in planes:
+            for half in halves:
+
+                def put(f, value, x=x, half=half):
+                    s1[f, x + 1, :, pl.ds(8 * half, 8), :] = value
+
+                advance(s0, cs, x, BASE0 + 8 * half, 8 * half, heat[0, half], put)
+
+    def z_arrived(group):
+        @pl.when(has_down)
+        def _():
+            z_copy(group, 0).wait_recv()
+
+        @pl.when(has_up)
+        def _():
+            z_copy(group, 1).wait_recv()
+
+    def first_rims(half, carry):
+        x_copy(0, 0, half).wait_recv()
+        x_copy(0, 1, half).wait_recv()
+        first_units((CX - 1, 0), (half,))
+        x_copy(1, 0, half).start()
+        x_copy(1, 1, half).start()
+
+        @pl.when(jnp.logical_and(half == 0, has_down))
+        def _():
+            for way, x in ((0, CX - 1), (1, 0)):
+                m_copy(x).start()
+                d_copy(way).start()
+
+        return carry
+
+    def first_step(m, carry):
+        xa = jnp.where(m < 5, 4 + 2 * m, jnp.where(m == 5, 2, 14))
+        xb = jnp.where(m < 6, xa + 1, 1)
+
+        @pl.when(jnp.logical_and(m < 5, lax.rem(m, 2) == 0))
+        def _():
+            z_arrived(1 + lax.div(m, 2))
+
+        @pl.when(m == 5)
+        def _():
+            z_arrived(0)
+            lax.fori_loop(0, 2, first_rims, 0)
+
+        first_units((xa, xb), (0, 1))
+
+        @pl.when(has_down)
+        def _():
+            m_copy(xa).start()
+            m_copy(xb).start()
+
+        return carry
+
+    lax.fori_loop(0, 7, first_step, 0)
+
+    def second_step(i, carry):
+        xa = jnp.where(i < 4, 5 + 2 * i, jnp.where(i < 6, 11 - 2 * i, jnp.where(i == 6, 13, 0)))
+        xb = jnp.where(i < 7, xa + 1, CX - 1)
+
+        @pl.when(jnp.logical_and(has_up, i == 0))
+        def _():
+            c_copy().wait_recv()
+            for x in range(4, 8):
+                m_copy(x).wait_recv()
+
+        @pl.when(jnp.logical_and(has_up, jnp.logical_and(i > 0, i < 7)))
+        def _():
+            first = jnp.where(jnp.logical_or(i < 4, i == 6), xa + 1, xa - 1)
+            m_copy(first).wait_recv()
+            m_copy(first + 1).wait_recv()
+
+        @pl.when(i == 7)
+        def _():
+            for half in range(2):
+                x_copy(1, 0, half).wait_recv()
+                x_copy(1, 1, half).wait_recv()
 
             @pl.when(has_up)
             def _():
-                z_copy(group, 1).wait_recv()
-
-        @pl.when(m == 6)
-        def _():
-            x_copy(0, 0, half).wait_recv()
-            x_copy(0, 1, half).wait_recv()
+                d_copy(0).wait_recv()
+                d_copy(1).wait_recv()
 
         for x in (xa, xb):
-
-            def put(f, value, x=x):
-                s1[f, x + 1, :, pl.ds(8 * half, 8), :] = value
-
-            advance(s0, cs, x, BASE0 + 8 * half, 8 * half, heat[0, half], put)
-
-        @pl.when(m == 6)
-        def _():
-            x_copy(1, 0, half).start()
-            x_copy(1, 1, half).start()
-
-        @pl.when(jnp.logical_and(half == 0, has_down))
-        def _():
-            m_copy(xa).start()
-            m_copy(xb).start()
-
-            @pl.when(m == 6)
-            def _():
-                d_copy(0).start()
-                d_copy(1).start()
-
+            for half in range(2):
+
+                def put(f, value, x=x, half=half):
+                    for k in range(YT):
+                        o[f, x, pl.ds(8 * half, 8), pl.ds(k * LANES, LANES)] = value[k]
+
+                advance(s1, cs, x, 1 + 8 * half, 1 + 8 * half, heat[1, half], put)
         return carry
 
-    lax.fori_loop(0, CX, first_step, 0)
-
-    def second_step(i, carry):
-        rim = i >= 14
-        half = jnp.where(rim, i - 14, lax.div(i, 7))
-        m = lax.rem(i, 7)
-        xa = jnp.where(rim, 0, jnp.where(m < 5, 5 + 2 * m, 13 - 2 * m))
-        xb = jnp.where(rim, CX - 1, xa + 1)
-
-        @pl.when(jnp.logical_and(has_up, i == 7))
-        def _():
-            c_copy().wait_recv()
-            m_copy(4).wait_recv()
-            m_copy(5).wait_recv()
-
-        @pl.when(jnp.logical_and(has_up, jnp.logical_and(i >= 7, i < 14)))
-        def _():
-            first = jnp.where(m < 5, xa + 1, xa - 1)
-            m_copy(first).wait_recv()
-            m_copy(first + 1).wait_recv()
-
-        @pl.when(i == 14)
-        def _():
-            for part in range(2):
-                x_copy(1, 0, part).wait_recv()
-                x_copy(1, 1, part).wait_recv()
-
-        @pl.when(jnp.logical_and(i == 15, has_up))
-        def _():
-            d_copy(0).wait_recv()
-            d_copy(1).wait_recv()
-
-        for x in (xa, xb):
-
-            def put(f, value, x=x):
-                for k in range(YT):
-                    o[f, x, pl.ds(pl.multiple_of(8 * half, 8), 8), pl.ds(k * LANES, LANES)] = value[k]
-
-            advance(s1, cs, x, 1 + 8 * half, 1 + 8 * half, heat[1, half], put)
-
-        @pl.when(jnp.logical_and(half == 1, jnp.logical_not(has_up)))
-        def _():
-            for x in (xa, xb):
-                o[:, x, pl.ds(CZ - 1, 1), :] = jnp.zeros((FIELDS, 1, NY), jnp.float32)
-
-        return carry
-
-    lax.fori_loop(0, CX, second_step, 0)
+    lax.fori_loop(0, 8, second_step, 0)
+
+    @pl.when(jnp.logical_not(has_up))
+    def _():
+        def clear_top(x, carry):
+            o[:, x, pl.ds(CZ - 1, 1), :] = jnp.zeros((FIELDS, 1, NY), jnp.float32)
+            return carry
+
+        lax.fori_loop(0, CX, clear_top, 0)
 
     for step in range(STEPS):
         for way in range(2):

time: 23.7 us -> 23.2 us (0.979)
  Pallas kernels: 22.8 us -> 22.4 us
    pallas_call x1, Pallas kernels: 21.3 us -> 20.9 us  [local(): pl.pallas_call(kernel, out_shape=pltpu.VMEM((FIELDS, CX, CZ, NY), jnp.flo...]
where the time goes in v4:
time: 23.2 us; the launch traced here: 23.1 us
  Pallas kernels  22.4 us (97%)
  between operations  0.64 us (3%)
    pallas_call x1, Pallas kernels, local(): pl.pallas_call(kernel, out_shape=pltpu.VMEM((FIELDS, CX, CZ, NY), jnp.flo...  20.9 us
    pallas_call x1, Pallas kernels, local(): pl.pallas_call(flush, out_shape=(pltpu.HBM(phase.shape, jnp.float32), plt...  1.5 us

profile of v4, /device:TPU:97, one launch (start us, length us, event | category | flops | bytes accessed | tf_op | source)
XLA Modules:
  0.0 23.1 jit_solution(9381186617957317256)
XLA Ops:
  0.6 20.9 %grow.1.o = f32[5,16,16,512]{3,2,1,0:T(8,128)S(1)} custom-call(s32[2]{0:T(128)} %frames_in.1, f32[4,16,16,512]{3,2,1,0:T(8,128)} %phase.1, f32[16,16,512]{2,1,0:T(8,128)} %solute.1, s32[4,16,16,512]{3,2,1,0:T(8,128)} %grain.1), custom_call_target="tpu_custom_call" | custom-call | tf_op jit(solution)/shard_map/grow/pallas_call | solution.py:417
  21.6 1.5 %flush.1 = (f32[4,16,16,512]{3,2,1,0:T(8,128)}, f32[16,16,512]{2,1,0:T(8,128)}) custom-call(f32[5,16,16,512]{3,2,1,0:T(8,128)S(1)} %grow.1.o), custom_call_target="tpu_custom_call" | custom-call | tf_op jit(solution)/shard_map/flush/pallas_call | solution.py:447

commit v5 on v4

--- a/solution.py
+++ b/solution.py
@@ -53,39 +53,48 @@
     return jnp.concatenate([rolled[-1:], rolled[:-1]], axis=0)
 
 
-def neighbours(s, f, xi, row):
+def neighbours(s, f, xi, row, part):
     at = pl.ds(row, 8)
-    c = s[f, xi, :, at, :]
-    xl = s[f, xi - 1, :, at, :]
-    xh = s[f, xi + 1, :, at, :]
-    zl = s[f, xi, :, pl.ds(row - 1, 8), :]
-    zh = s[f, xi, :, pl.ds(row + 1, 8), :]
+    ys = slice(None) if part is None else pl.ds(2 * part, 2)
+    c = s[f, xi, ys, at, :]
+    xl = s[f, xi - 1, ys, at, :]
+    xh = s[f, xi + 1, ys, at, :]
+    zl = s[f, xi, ys, pl.ds(row - 1, 8), :]
+    zh = s[f, xi, ys, pl.ds(row + 1, 8), :]
     lane = lax.broadcasted_iota(jnp.int32, c.shape, 2)
     right = pltpu.roll(c, 1, axis=2)
     left = pltpu.roll(c, LANES - 1, axis=2)
-    yl = jnp.where(lane == 0, next_y(right, -1), right)
-    yh = jnp.where(lane == LANES - 1, next_y(left, 1), left)
+    if part is None:
+        before, after = next_y(right, -1), next_y(left, 1)
+    else:
+        before = s[f, xi, pl.ds(lax.rem(2 * part + YT - 1, YT), 1), at, :]
+        after = s[f, xi, pl.ds(lax.rem(2 * part + 2, YT), 1), at, :]
+        before = jnp.concatenate([pltpu.roll(before, 1, axis=2), right[:1]], axis=0)
+        after = jnp.concatenate([left[1:], pltpu.roll(after, LANES - 1, axis=2)], axis=0)
+    yl = jnp.where(lane == 0, before, right)
+    yh = jnp.where(lane == LANES - 1, after, left)
     return c, xl, xh, yl, yh, zl, zh
 
 
-def advance(s, cs, x, row, cs_row, thermal, put):
+def advance(s, cs, x, row, cs_row, thermal, put, part=None):
     xi = x + 1
-    u = s[ORDERS, xi, :, pl.ds(row, 8), :]
+    ys = slice(None) if part is None else pl.ds(2 * part, 2)
+    u = s[ORDERS, xi, ys, pl.ds(row, 8), :]
     drive = thermal - 2.4 * u
     q = None
     for k in range(ORDERS):
-        p = s[k, xi, :, pl.ds(row, 8), :]
+        p = s[k, xi, ys, pl.ds(row, 8), :]
         q = p * p if q is None else q + p * p
     well = 0.64 - 0.16 * q
     total = None
     for k in range(ORDERS):
-        p, xl, xh, yl, yh, zl, zh = neighbours(s, k, xi, row)
+        p, xl, xh, yl, yh, zl, zh = neighbours(s, k, xi, row, part)
         gx, gy, gz = xh - xl, yh - yl, zh - zl
         lap = (xl + xh) + (yl + yh) + (zl + zh) - 6.0 * p
         x2, y2, z2 = gx * gx, gy * gy, gz * gz
         r = x2 + y2
         at = pl.ds(cs_row, 8)
-        t = cs[0, k, x, :, at, :] * (gx * gy) + cs[1, k, x, :, at, :] * (x2 - y2)
+        t = cs[0, k, x, ys, at, :] * (gx * gy) + cs[1, k, x, ys, at, :] * (x2 - y2)
         quartic = r * r + z2 * z2 - t * t
         d = (r + z2) + 0.2
         ratio = quartic * pl.reciprocal(d * d, approx=True)
@@ -97,14 +106,35 @@
         )
         put(k, p + delta)
         total = delta if total is None else total + delta
-    c, xl, xh, yl, yh, zl, zh = neighbours(s, ORDERS, xi, row)
+    c, xl, xh, yl, yh, zl, zh = neighbours(s, ORDERS, xi, row, part)
     near = (xl + xh) + (yl + yh) + (zl + zh)
     put(ORDERS, 0.52 * c + 0.08 * near + 0.5 * total)
 
 
+def second_units(o, s1, cs, heat, planes, first):
+    for x in planes:
+        for half in range(2):
+
+            def put(f, value, x=x, half=half):
+                for k in range(YT):
+                    o[f, x - first, pl.ds(8 * half, 8), pl.ds(k * LANES, LANES)] = value[k]
+
+            advance(s1, cs, x, 1 + 8 * half, 1 + 8 * half, heat[1, half], put)
+
+
+def clear_top(o, has_up):
+    @pl.when(jnp.logical_not(has_up))
+    def _():
+        def clear(x, carry):
+            o[:, x, pl.ds(CZ - 1, 1), :] = jnp.zeros((FIELDS, 1, NY), jnp.float32)
+            return carry
+
+        lax.fori_loop(0, o.shape[1], clear, 0)
+
+
 def kernel(
-    frames_in, phase, solute, grain, o,
-    s0, s1, g, cs, heat, frames,
+    frames_in, phase, solute, grain, o, s1, cs, heat,
+    s0, g, frames,
     load_sem, frame_sem, x_send, x_recv, z_send, z_recv, m_send, m_recv, c_send, c_recv, d_send, d_recv,
 ):
     gx, gz = lax.axis_index("gx"), lax.axis_index("gz")
@@ -178,15 +208,16 @@
             src_ref=src, dst_ref=dst, send_sem=send, recv_sem=recv, device_id=(ix, iz), device_id_type=MESH
         )
 
-    def x_copy(step, way, half):
+    def x_copy(step, way, piece):
         s, base = (s0, BASE0) if step == 0 else (s1, 0)
-        rows = pl.ds(base + 8 * half, 8)
+        half, part = lax.div(piece, 2), lax.rem(piece, 2)
+        ys, rows = pl.ds(2 * part, 2), pl.ds(base + 8 * half, 8)
         src, dst, to = (CX, 0, right) if way == 0 else (1, CX + 1, left)
         return remote(
-            s.at[:, src, :, rows, :],
-            s.at[:, dst, :, rows, :],
-            x_send.at[step, way, half],
-            x_recv.at[step, way, half],
+            s.at[:, src, ys, rows, :],
+            s.at[:, dst, ys, rows, :],
+            x_send.at[step, way, piece],
+            x_recv.at[step, way, piece],
             to,
             gz,
         )
@@ -235,9 +266,9 @@
 
     pl.semaphore_wait(barrier, 2 + has_up.astype(jnp.int32) + has_down.astype(jnp.int32))
 
-    for half in range(2):
-        x_copy(0, 0, half).start()
-        x_copy(0, 1, half).start()
+    for piece in range(4):
+        x_copy(0, 0, piece).start()
+        x_copy(0, 1, piece).start()
     for group in (1, 2, 3, 0):
 
         @pl.when(has_up)
@@ -292,14 +323,20 @@
         def _():
             z_copy(group, 1).wait_recv()
 
-    def first_rims(half, carry):
-        x_copy(0, 0, half).wait_recv()
-        x_copy(0, 1, half).wait_recv()
-        first_units((CX - 1, 0), (half,))
-        x_copy(1, 0, half).start()
-        x_copy(1, 1, half).start()
-
-        @pl.when(jnp.logical_and(half == 0, has_down))
+    def first_rims(piece, carry):
+        half, part = lax.div(piece, 2), lax.rem(piece, 2)
+        x_copy(0, 0, piece).wait_recv()
+        x_copy(0, 1, piece).wait_recv()
+        for x in (CX - 1, 0):
+
+            def put(f, value, x=x):
+                s1[f, x + 1, pl.ds(2 * part, 2), pl.ds(pl.multiple_of(8 * half, 8), 8), :] = value
+
+            advance(s0, cs, x, BASE0 + 8 * half, 8 * half, heat[0, half], put, part)
+        x_copy(1, 0, piece).start()
+        x_copy(1, 1, piece).start()
+
+        @pl.when(jnp.logical_and(piece == 1, has_down))
         def _():
             for way, x in ((0, CX - 1), (1, 0)):
                 m_copy(x).start()
@@ -318,7 +355,7 @@
         @pl.when(m == 5)
         def _():
             z_arrived(0)
-            lax.fori_loop(0, 2, first_rims, 0)
+            lax.fori_loop(0, 4, first_rims, 0)
 
         first_units((xa, xb), (0, 1))
 
@@ -332,8 +369,7 @@
     lax.fori_loop(0, 7, first_step, 0)
 
     def second_step(i, carry):
-        xa = jnp.where(i < 4, 5 + 2 * i, jnp.where(i < 6, 11 - 2 * i, jnp.where(i == 6, 13, 0)))
-        xb = jnp.where(i < 7, xa + 1, CX - 1)
+        xa = jnp.where(i < 4, 5 + 2 * i, jnp.where(i < 6, 11 - 2 * i, 13))
 
         @pl.when(jnp.logical_and(has_up, i == 0))
         def _():
@@ -341,47 +377,21 @@
             for x in range(4, 8):
                 m_copy(x).wait_recv()
 
-        @pl.when(jnp.logical_and(has_up, jnp.logical_and(i > 0, i < 7)))
+        @pl.when(jnp.logical_and(has_up, i > 0))
         def _():
             first = jnp.where(jnp.logical_or(i < 4, i == 6), xa + 1, xa - 1)
             m_copy(first).wait_recv()
             m_copy(first + 1).wait_recv()
 
-        @pl.when(i == 7)
-        def _():
-            for half in range(2):
-                x_copy(1, 0, half).wait_recv()
-                x_copy(1, 1, half).wait_recv()
-
-            @pl.when(has_up)
-            def _():
-                d_copy(0).wait_recv()
-                d_copy(1).wait_recv()
-
-        for x in (xa, xb):
-            for half in range(2):
-
-                def put(f, value, x=x, half=half):
-                    for k in range(YT):
-                        o[f, x, pl.ds(8 * half, 8), pl.ds(k * LANES, LANES)] = value[k]
-
-                advance(s1, cs, x, 1 + 8 * half, 1 + 8 * half, heat[1, half], put)
+        second_units(o, s1, cs, heat, (xa, xa + 1), 0)
         return carry
 
-    lax.fori_loop(0, 8, second_step, 0)
-
-    @pl.when(jnp.logical_not(has_up))
-    def _():
-        def clear_top(x, carry):
-            o[:, x, pl.ds(CZ - 1, 1), :] = jnp.zeros((FIELDS, 1, NY), jnp.float32)
-            return carry
-
-        lax.fori_loop(0, CX, clear_top, 0)
-
-    for step in range(STEPS):
-        for way in range(2):
-            for half in range(2):
-                x_copy(step, way, half).wait_send()
+    lax.fori_loop(0, 7, second_step, 0)
+    clear_top(o, has_up)
+
+    for way in range(2):
+        for piece in range(4):
+            x_copy(0, way, piece).wait_send()
 
     @pl.when(has_up)
     def _():
@@ -398,14 +408,35 @@
         d_copy(0).wait_send()
         d_copy(1).wait_send()
 
-
-def flush(o, phase_out, solute_out, sem):
-    copies = (
-        pltpu.make_async_copy(o.at[pl.ds(0, ORDERS)], phase_out, sem.at[0]),
-        pltpu.make_async_copy(o.at[ORDERS], solute_out, sem.at[1]),
-    )
+    @pl.when(has_up)
+    def _():
+        d_copy(0).wait_recv()
+        d_copy(1).wait_recv()
+
+    for way in range(2):
+        for piece in range(4):
+            x_copy(1, way, piece).wait()
+
+
+def finish(o, s1, cs, heat, phase_out, solute_out, rims, sem):
+    inner = pl.ds(1, CX - 2)
+    copies = [
+        pltpu.make_async_copy(o.at[pl.ds(0, ORDERS), inner], phase_out.at[:, inner], sem.at[0]),
+        pltpu.make_async_copy(o.at[ORDERS, inner], solute_out.at[inner], sem.at[1]),
+    ]
     for copy in copies:
         copy.start()
+    for i, x in enumerate((0, CX - 1)):
+        second_units(rims.at[:, pl.ds(i, 1)], s1, cs, heat, (x,), x)
+    clear_top(rims, lax.axis_index("gz") < lax.axis_size("gz") - 1)
+    for i, x in enumerate((0, CX - 1)):
+        ends = [
+            pltpu.make_async_copy(rims.at[pl.ds(0, ORDERS), i], phase_out.at[:, x], sem.at[2 + 2 * i]),
+            pltpu.make_async_copy(rims.at[ORDERS, i], solute_out.at[x], sem.at[3 + 2 * i]),
+        ]
+        for copy in ends:
+            copy.start()
+        copies += ends
     for copy in copies:
         copy.wait()
 
@@ -414,22 +445,24 @@
     hbm, vmem = pl.BlockSpec(memory_space=pltpu.HBM), pl.BlockSpec(memory_space=pltpu.VMEM)
     dma = pltpu.SemaphoreType.DMA
     args = [pltpu.with_memory_space_constraint(a, pltpu.HBM) for a in (frame_steps, phase, solute, grain_map)]
-    result = pl.pallas_call(
+    results = pl.pallas_call(
         kernel,
-        out_shape=pltpu.VMEM((FIELDS, CX, CZ, NY), jnp.float32),
+        out_shape=(
+            pltpu.VMEM((FIELDS, CX, CZ, NY), jnp.float32),
+            pltpu.VMEM((FIELDS, CX + 2, YT, 24, LANES), jnp.float32),
+            pltpu.VMEM((2, ORDERS, CX, YT, 24, LANES), jnp.float32),
+            pltpu.VMEM((STEPS, 2, 1, 8, LANES), jnp.float32),
+        ),
         in_specs=[hbm] * 4,
-        out_specs=vmem,
+        out_specs=(vmem,) * 4,
         scratch_shapes=[
             pltpu.VMEM((FIELDS, CX + 2, YT, 32, LANES), jnp.float32),
-            pltpu.VMEM((FIELDS, CX + 2, YT, 24, LANES), jnp.float32),
             pltpu.VMEM((ORDERS, CX, YT, CZ, LANES), jnp.int32),
-            pltpu.VMEM((2, ORDERS, CX, YT, 24, LANES), jnp.float32),
-            pltpu.VMEM((STEPS, 2, 1, 8, LANES), jnp.float32),
             pltpu.SMEM((STEPS,), jnp.int32),
             dma((3, YT)),
             dma,
-            dma((STEPS, 2, 2)),
-            dma((STEPS, 2, 2)),
+            dma((STEPS, 2, 4)),
+            dma((STEPS, 2, 4)),
             dma((2, GROUPS)),
             dma((2, GROUPS)),
             dma((CX,)),
@@ -445,17 +478,17 @@
         name="grow",
     )(*args)
     return pl.pallas_call(
-        flush,
+        finish,
         out_shape=(
             pltpu.HBM(phase.shape, jnp.float32),
             pltpu.HBM(solute.shape, jnp.float32),
         ),
-        in_specs=[vmem],
+        in_specs=[vmem] * 4,
         out_specs=(hbm, hbm),
-        scratch_shapes=[dma((2,))],
-        compiler_params=pltpu.CompilerParams(vmem_limit_bytes=4 * 1024 * 1024),
-        name="flush",
-    )(result)
+        scratch_shapes=[pltpu.VMEM((FIELDS, 2, CZ, NY), jnp.float32), dma((6,))],
+        compiler_params=pltpu.CompilerParams(vmem_limit_bytes=16 * 1024 * 1024),
+        name="finish",
+    )(*results)
 
 
 def solution(mesh):

time: 23.2 us -> 22.9 us (0.987)
    pallas_call x2, Pallas kernels: 22.4 us -> 22.2 us  [the longest x1 20.5 us: local(): pl.pallas_call(kernel, out_shape=(pltpu.VMEM((FIELDS, CX, CZ, NY), jnp.fl...]
where the time goes in v5:
time: 22.9 us; the launch traced here: 22.8 us
  Pallas kernels  22.2 us (97%)
  between operations  0.64 us (3%)
    pallas_call x1, Pallas kernels, local(): pl.pallas_call(kernel, out_shape=(pltpu.VMEM((FIELDS, CX, CZ, NY), jnp.fl...  20.5 us
    pallas_call x1, Pallas kernels, local(): pl.pallas_call(finish, out_shape=(pltpu.HBM(phase.shape, jnp.float32), pl...  1.74 us

profile of v5, /device:TPU:97, one launch (start us, length us, event | category | flops | bytes accessed | tf_op | source)
XLA Modules:
  0.0 22.8 jit_solution(14043938012434023744)
XLA Ops:
  0.6 20.5 %grow.1 = (f32[5,16,16,512]{3,2,1,0:T(8,128)S(1)}, f32[5,18,4,24,128]{4,3,2,1,0:T(8,128)S(1)}, f32[2,4,16,4,24,128]{5,4,3,2,1,0:T(8,128)S(1)}, f32[2,2,1,8,128]{4,3,2,1,0:T(8,128)S(1)}) custom-call(s32[2]{0:T(128)} %frames_in.1, f32[4,16,16,512]{3,2,1,0:T(8,128)} %phase.1, f32[16,16,512]{2,1,0:T(8,128)} %solute.1, s32[4,16,16,512]{3,2,1,0:T(8,128)} %grain.1), custom_call_target="tpu_custom_call" | custom-call | tf_op jit(solution)/shard_map/grow/pallas_call | solution.py:448
  21.1 1.7 %finish.1 = (f32[4,16,16,512]{3,2,1,0:T(8,128)}, f32[16,16,512]{2,1,0:T(8,128)}) custom-call(f32[5,16,16,512]{3,2,1,0:T(8,128)S(1)} %get-tuple-element.6.o, f32[5,18,4,24,128]{4,3,2,1,0:T(8,128)S(1)} %get-tuple-element.7.s1, f32[2,4,16,4,24,128]{5,4,3,2,1,0:T(8,128)S(1)} %get-tuple-element.8.cs, f32[2,2,1,8,128]{4,3,2,1,0:T(8,128)S(1)} %get-tuple-element.9.heat), custom_call_target="tpu_custom_call" | custom-call | tf_op jit(solution)/shard_map/finish/pallas_call | solution.py:480

commit v6 on v5

--- a/solution.py
+++ b/solution.py
@@ -23,6 +23,8 @@
 MESH = pl.DeviceIdType.MESH
 
 BASE0 = 8
+
+RIMS_AT = 5
 
 
 def sine_coefficients():
@@ -111,15 +113,18 @@
     put(ORDERS, 0.52 * c + 0.08 * near + 0.5 * total)
 
 
-def second_units(o, s1, cs, heat, planes, first):
-    for x in planes:
-        for half in range(2):
-
-            def put(f, value, x=x, half=half):
-                for k in range(YT):
-                    o[f, x - first, pl.ds(8 * half, 8), pl.ds(k * LANES, LANES)] = value[k]
-
-            advance(s1, cs, x, 1 + 8 * half, 1 + 8 * half, heat[1, half], put)
+def tile(half):
+    return pl.ds(8 * half if isinstance(half, int) else pl.multiple_of(8 * half, 8), 8)
+
+
+def second_units(o, s1, cs, heat, units, first):
+    for x, half in units:
+
+        def put(f, value, x=x, half=half):
+            for k in range(YT):
+                o[f, x - first, tile(half), pl.ds(k * LANES, LANES)] = value[k]
+
+        advance(s1, cs, x, 1 + 8 * half, 1 + 8 * half, heat[1, half], put)
 
 
 def clear_top(o, has_up):
@@ -305,23 +310,20 @@
             height = (NZ // 2 - z - frames[step]).astype(jnp.float32)
             heat[step, half] = 2.4 * jnp.tanh(height * 0.125)
 
-    def first_units(planes, halves):
-        for x in planes:
-            for half in halves:
-
-                def put(f, value, x=x, half=half):
-                    s1[f, x + 1, :, pl.ds(8 * half, 8), :] = value
-
-                advance(s0, cs, x, BASE0 + 8 * half, 8 * half, heat[0, half], put)
-
-    def z_arrived(group):
-        @pl.when(has_down)
-        def _():
-            z_copy(group, 0).wait_recv()
-
-        @pl.when(has_up)
-        def _():
-            z_copy(group, 1).wait_recv()
+    def first_units(units):
+        for x, half in units:
+
+            def put(f, value, x=x, half=half):
+                s1[f, x + 1, :, tile(half), :] = value
+
+            advance(s0, cs, x, BASE0 + 8 * half, 8 * half, heat[0, half], put)
+
+    def units_of(group, lower, upper):
+        xa = jnp.where(group < 3, 4 + 4 * group, 14)
+        xb = jnp.where(group < 3, xa + 1, 1)
+        xc = jnp.where(group < 2, xa + 2, jnp.where(group == 2, 2, 14))
+        xd = jnp.where(group < 3, xc + 1, 1)
+        return ((xa, lower), (xb, lower), (xc, upper), (xd, upper))
 
     def first_rims(piece, carry):
         half, part = lax.div(piece, 2), lax.rem(piece, 2)
@@ -330,7 +332,7 @@
         for x in (CX - 1, 0):
 
             def put(f, value, x=x):
-                s1[f, x + 1, pl.ds(2 * part, 2), pl.ds(pl.multiple_of(8 * half, 8), 8), :] = value
+                s1[f, x + 1, pl.ds(2 * part, 2), tile(half), :] = value
 
             advance(s0, cs, x, BASE0 + 8 * half, 8 * half, heat[0, half], put, part)
         x_copy(1, 0, piece).start()
@@ -344,46 +346,67 @@
 
         return carry
 
-    def first_step(m, carry):
-        xa = jnp.where(m < 5, 4 + 2 * m, jnp.where(m == 5, 2, 14))
-        xb = jnp.where(m < 6, xa + 1, 1)
-
-        @pl.when(jnp.logical_and(m < 5, lax.rem(m, 2) == 0))
-        def _():
-            z_arrived(1 + lax.div(m, 2))
-
-        @pl.when(m == 5)
-        def _():
-            z_arrived(0)
+    def first_step(i, carry):
+        group = jnp.where(i < 4, i, i - 4)
+
+        @pl.when(jnp.logical_and(has_down, i < 3))
+        def _():
+            z_copy(i + 1, 0).wait_recv()
+
+        @pl.when(jnp.logical_and(has_down, i == 2))
+        def _():
+            z_copy(0, 0).wait_recv()
+
+        @pl.when(jnp.logical_and(has_up, i == 3))
+        def _():
+            for every in (1, 2, 3, 0):
+                z_copy(every, 1).wait_recv()
+
+        @pl.when(i == RIMS_AT)
+        def _():
             lax.fori_loop(0, 4, first_rims, 0)
 
-        first_units((xa, xb), (0, 1))
-
-        @pl.when(has_down)
-        def _():
-            m_copy(xa).start()
-            m_copy(xb).start()
+        units = units_of(group, lax.div(i, 4), jnp.where(i < 3, 0, 1))
+        first_units(units)
+
+        @pl.when(jnp.logical_and(has_down, i < 4))
+        def _():
+            m_copy(units[0][0]).start()
+            m_copy(units[1][0]).start()
+
+            @pl.when(i < 3)
+            def _():
+                m_copy(units[2][0]).start()
+                m_copy(units[3][0]).start()
 
         return carry
 
     lax.fori_loop(0, 7, first_step, 0)
 
     def second_step(i, carry):
-        xa = jnp.where(i < 4, 5 + 2 * i, jnp.where(i < 6, 11 - 2 * i, 13))
-
-        @pl.when(jnp.logical_and(has_up, i == 0))
+        @pl.when(jnp.logical_and(has_up, i == 3))
         def _():
             c_copy().wait_recv()
-            for x in range(4, 8):
+            for x in range(3, 9):
                 m_copy(x).wait_recv()
 
-        @pl.when(jnp.logical_and(has_up, i > 0))
-        def _():
-            first = jnp.where(jnp.logical_or(i < 4, i == 6), xa + 1, xa - 1)
-            m_copy(first).wait_recv()
-            m_copy(first + 1).wait_recv()
-
-        second_units(o, s1, cs, heat, (xa, xa + 1), 0)
+        @pl.when(jnp.logical_and(has_up, i == 4))
+        def _():
+            for x in range(9, 13):
+                m_copy(x).wait_recv()
+
+        @pl.when(jnp.logical_and(has_up, i == 5))
+        def _():
+            for x in (13, 14, 1, 2):
+                m_copy(x).wait_recv()
+
+        @pl.when(jnp.logical_and(has_up, i == 6))
+        def _():
+            m_copy(CX - 1).wait_recv()
+            m_copy(0).wait_recv()
+
+        group = jnp.where(i < 3, i, i - 3)
+        second_units(o, s1, cs, heat, units_of(group, jnp.where(jnp.logical_and(i >= 3, i < 6), 1, 0), jnp.where(i < 3, 0, 1)), 0)
         return carry
 
     lax.fori_loop(0, 7, second_step, 0)
@@ -427,7 +450,7 @@
     for copy in copies:
         copy.start()
     for i, x in enumerate((0, CX - 1)):
-        second_units(rims.at[:, pl.ds(i, 1)], s1, cs, heat, (x,), x)
+        second_units(rims.at[:, pl.ds(i, 1)], s1, cs, heat, ((x, 0), (x, 1)), x)
     clear_top(rims, lax.axis_index("gz") < lax.axis_size("gz") - 1)
     for i, x in enumerate((0, CX - 1)):
         ends = [

time: 22.9 us -> 23 us (level)
  no operation moved by 1% of the time
where the time goes in v6:
time: 23 us; the launch traced here: 22.9 us
  Pallas kernels  22.3 us (97%)
  between operations  0.64 us (3%)
    pallas_call x1, Pallas kernels, local(): pl.pallas_call(kernel, out_shape=(pltpu.VMEM((FIELDS, CX, CZ, NY), jnp.fl...  20.6 us
    pallas_call x1, Pallas kernels, local(): pl.pallas_call(finish, out_shape=(pltpu.HBM(phase.shape, jnp.float32), pl...  1.74 us

profile of v6, /device:TPU:97, one launch (start us, length us, event | category | flops | bytes accessed | tf_op | source)
XLA Modules:
  0.0 22.9 jit_solution(15168193192079256336)
XLA Ops:
  0.6 20.6 %grow.1 = (f32[5,16,16,512]{3,2,1,0:T(8,128)S(1)}, f32[5,18,4,24,128]{4,3,2,1,0:T(8,128)S(1)}, f32[2,4,16,4,24,128]{5,4,3,2,1,0:T(8,128)S(1)}, f32[2,2,1,8,128]{4,3,2,1,0:T(8,128)S(1)}) custom-call(s32[2]{0:T(128)} %frames_in.1, f32[4,16,16,512]{3,2,1,0:T(8,128)} %phase.1, f32[16,16,512]{2,1,0:T(8,128)} %solute.1, s32[4,16,16,512]{3,2,1,0:T(8,128)} %grain.1), custom_call_target="tpu_custom_call" | custom-call | tf_op jit(solution)/shard_map/grow/pallas_call | solution.py:471
  21.2 1.7 %finish.1 = (f32[4,16,16,512]{3,2,1,0:T(8,128)}, f32[16,16,512]{2,1,0:T(8,128)}) custom-call(f32[5,16,16,512]{3,2,1,0:T(8,128)S(1)} %get-tuple-element.6.o, f32[5,18,4,24,128]{4,3,2,1,0:T(8,128)S(1)} %get-tuple-element.7.s1, f32[2,4,16,4,24,128]{5,4,3,2,1,0:T(8,128)S(1)} %get-tuple-element.8.cs, f32[2,2,1,8,128]{4,3,2,1,0:T(8,128)S(1)} %get-tuple-element.9.heat), custom_call_target="tpu_custom_call" | custom-call | tf_op jit(solution)/shard_map/finish/pallas_call | solution.py:503

commit v7 on v6

v7 whole, which is shorter than its diff:
```python
import math

import jax
import jax.numpy as jnp
import numpy as np
from jax import lax
from jax.experimental import pallas as pl
from jax.experimental.pallas import tpu as pltpu
from jax.sharding import PartitionSpec as P

ORDERS = 4
FIELDS = 5
STEPS = 2
NGRAIN = 1024
NZ = 256
CX = 16
CZ = 16
NY = 512
LANES = 128
YT = NY // LANES
GROUP = 4
GROUPS = CX // GROUP
MESH = pl.DeviceIdType.MESH

BASE0 = 8

RIMS_AT = 5


def sine_coefficients():
    nodes = np.cos(np.pi * (np.arange(400) + 0.5) / 400)
    theta = nodes * np.pi / 2
    even = np.polynomial.chebyshev.Chebyshev.fit(nodes, np.cos(theta), 8, domain=[-1, 1])
    odd = np.polynomial.chebyshev.Chebyshev.fit(nodes, np.sin(theta), 9, domain=[-1, 1])
    even = even.convert(kind=np.polynomial.Polynomial).coef
    odd = odd.convert(kind=np.polynomial.Polynomial).coef
    cos_c = [float(even[i] * math.sqrt(0.5) / 128.0**i) for i in (0, 2, 4, 6, 8)]
    sin_c = [float(odd[i] * math.sqrt(2.0) / 128.0**i) for i in (1, 3, 5, 7, 9)]
    return sin_c, cos_c


SIN_C, COS_C = sine_coefficients()


def horner(x, coefficients):
    value = coefficients[-1]
    for c in coefficients[-2::-1]:
        value = value * x + c
    return value


def next_y(rolled, offset):
    if offset > 0:
        return jnp.concatenate([rolled[1:], rolled[:1]], axis=0)
    return jnp.concatenate([rolled[-1:], rolled[:-1]], axis=0)


def neighbours(s, f, xi, row):
    at = pl.ds(row, 8)
    c = s[f, xi, :, at, :]
    xl = s[f, xi - 1, :, at, :]
    xh = s[f, xi + 1, :, at, :]
    zl = s[f, xi, :, pl.ds(row - 1, 8), :]
    zh = s[f, xi, :, pl.ds(row + 1, 8), :]
    lane = lax.broadcasted_iota(jnp.int32, c.shape, 2)
    right = pltpu.roll(c, 1, axis=2)
    left = pltpu.roll(c, LANES - 1, axis=2)
    yl = jnp.where(lane == 0, next_y(right, -1), right)
    yh = jnp.where(lane == LANES - 1, next_y(left, 1), left)
    return c, xl, xh, yl, yh, zl, zh


def advance(s, xi, row, cs, ci, cs_row, thermal, put):
    u = s[ORDERS, xi, :, pl.ds(row, 8), :]
    drive = thermal - 2.4 * u
    q = None
    for k in range(ORDERS):
        p = s[k, xi, :, pl.ds(row, 8), :]
        q = p * p if q is None else q + p * p
    well = 0.64 - 0.16 * q
    total = None
    for k in range(ORDERS):
        p, xl, xh, yl, yh, zl, zh = neighbours(s, k, xi, row)
        gx, gy, gz = xh - xl, yh - yl, zh - zl
        lap = (xl + xh) + (yl + yh) + (zl + zh) - 6.0 * p
        x2, y2, z2 = gx * gx, gy * gy, gz * gz
        r = x2 + y2
        at = pl.ds(cs_row, 8)
        t = cs[0, k, ci, :, at, :] * (gx * gy) + cs[1, k, ci, :, at, :] * (x2 - y2)
        quartic = r * r + z2 * z2 - t * t
        d = (r + z2) + 0.2
        ratio = quartic * pl.reciprocal(d * d, approx=True)
        w = p - p * p
        delta = (
            lap * (0.08 + 0.04 * ratio)
            + p * (well + p * (1.44 * p - 1.92))
            + (w * w) * drive
        )
        put(k, p + delta)
        total = delta if total is None else total + delta
    c, xl, xh, yl, yh, zl, zh = neighbours(s, ORDERS, xi, row)
    near = (xl + xh) + (yl + yh) + (zl + zh)
    put(ORDERS, 0.52 * c + 0.08 * near + 0.5 * total)


def tile(half):
    return pl.ds(8 * half if isinstance(half, int) else pl.multiple_of(8 * half, 8), 8)


def first_units(s0, s1, cs, heat, units):
    for x, half in units:

        def put(f, value, x=x, half=half):
            s1[f, x + 1, :, tile(half), :] = value

        advance(s0, x + 2, BASE0 + 8 * half, cs, x + 1, 8 * half, heat[0, half], put)


def second_units(o, s1, cs, heat, units, first):
    for x, half in units:

        def put(f, value, x=x, half=half):
            for k in range(YT):
                o[f, x - first, tile(half), pl.ds(k * LANES, LANES)] = value[k]

        advance(s1, x + 1, 1 + 8 * half, cs, x + 1, 1 + 8 * half, heat[1, half], put)


def clear_top(o, has_up):
    @pl.when(jnp.logical_not(has_up))
    def _():
        def clear(x, carry):
            o[:, x, pl.ds(CZ - 1, 1), :] = jnp.zeros((FIELDS, 1, NY), jnp.float32)
            return carry

        lax.fori_loop(0, o.shape[1], clear, 0)


def store_trig(cs, k, ci, at, ys, grain):
    h = ((grain & 255) - 128).astype(jnp.float32)
    h2 = h * h
    cs[0, k, ci, ys, at, :] = h * horner(h2, SIN_C)
    cs[1, k, ci, ys, at, :] = horner(h2, COS_C)


def kernel(
    frames_in, phase, solute, grain, o, s1, cs, heat,
    s0, g, xh, gh, frames,
    load_sem, frame_sem, near_sem, x_send, x_recv, z_send, z_recv, m_send, m_recv, c_send, c_recv, f_send, f_recv,
):
    gx, gz = lax.axis_index("gx"), lax.axis_index("gz")
    n_gx, n_gz = lax.axis_size("gx"), lax.axis_size("gz")
    right, left = lax.rem(gx + 1, n_gx), lax.rem(gx + n_gx - 1, n_gx)
    has_up, has_down = gz < n_gz - 1, gz > 0

    barrier = pltpu.get_barrier_semaphore()

    def greet(ix, iz):
        pl.semaphore_signal(barrier, inc=1, device_id=(ix, iz), device_id_type=MESH)

    greet(left, gz)

    @pl.when(has_up)
    def _():
        greet(gx, gz + 1)

    @pl.when(has_down)
    def _():
        greet(gx, gz - 1)

    loads = []
    for k in range(YT):
        lanes = pl.ds(k * LANES, LANES)
        rows = pl.ds(BASE0, CZ)
        loads.append(
            (
                pltpu.make_async_copy(
                    phase.at[:, :, :, lanes], s0.at[pl.ds(0, ORDERS), pl.ds(2, CX), k, rows, :], load_sem.at[0, k]
                ),
                pltpu.make_async_copy(
                    solute.at[:, :, lanes], s0.at[ORDERS, pl.ds(2, CX), k, rows, :], load_sem.at[1, k]
                ),
                pltpu.make_async_copy(grain.at[:, :, :, lanes], g.at[:, :, k, :, :], load_sem.at[2, k]),
            )
        )
    frame_load = pltpu.make_async_copy(frames_in, frames, frame_sem)
    for which in range(3):
        for k in range(YT):
            loads[k][which].start()
    frame_load.start()

    def remote(src, dst, send, recv, ix, iz):
        return pltpu.make_async_remote_copy(
            src_ref=src, dst_ref=dst, send_sem=send, recv_sem=recv, device_id=(ix, iz), device_id_type=MESH
        )

    def x_copy(way, i):
        outer, inner, to = (CX - 1, CX - 2, right) if way == 0 else (0, 1, left)
        orders = pl.ds(0, ORDERS)
        src, dst = (
            (phase.at[:, outer], xh.at[way, 0, orders]),
            (solute.at[outer], xh.at[way, 0, ORDERS]),
            (grain.at[:, outer], gh.at[way]),
            (phase.at[:, inner], xh.at[way, 1, orders]),
            (solute.at[inner], xh.at[way, 1, ORDERS]),
        )[i]
        return remote(src, dst, x_send.at[way, i], x_recv.at[way, i], to, gz)

    def z_copy(group, way):
        planes = pl.ds(2 + group * GROUP, GROUP)
        if way == 0:
            src, dst, to = pl.ds(BASE0 + CZ - 1, 1), pl.ds(BASE0 - 1, 1), gz + 1
        else:
            deep = 2 if group in (0, GROUPS - 1) else 1
            src, dst, to = pl.ds(BASE0, deep), pl.ds(BASE0 + CZ, deep), gz - 1
        return remote(
            s0.at[:, planes, :, src, :], s0.at[:, planes, :, dst, :], z_send.at[way, group], z_recv.at[way, group], gx, to
        )

    def m_copy(x):
        return remote(
            s1.at[:, x + 1, :, pl.ds(0, 2), :],
            s1.at[:, x + 1, :, pl.ds(CZ, 2), :],
            m_send.at[x],
            m_recv.at[x],
            gx,
            gz - 1,
        )

    def c_copy(part):
        planes = (pl.ds(1, 1), pl.ds(CX, 1), pl.ds(2, CX - 2))[part]
        return remote(
            cs.at[:, :, planes, :, pl.ds(0, 1), :],
            cs.at[:, :, planes, :, pl.ds(CZ, 1), :],
            c_send.at[part],
            c_recv.at[part],
            gx,
            gz - 1,
        )

    def f_copy(what, way):
        to = right if way == 0 else left
        if what == 1:
            src, dst = (CX, 0) if way == 0 else (1, CX + 1)
            at = pl.ds(CZ, 1)
            pair = cs.at[:, :, src, :, at, :], cs.at[:, :, dst, :, at, :]
        else:
            src, dst = (CX, 0) if way == 0 else (2, CX + 2)
            at = pl.ds(BASE0 + CZ, 2) if what == 0 else pl.ds(BASE0 - 1, 1)
            pair = s0.at[:, pl.ds(src, 2), :, at, :], s0.at[:, pl.ds(dst, 2), :, at, :]
        return remote(*pair, f_send.at[what, way], f_recv.at[what, way], to, gz)

    def towards_left():
        pl.semaphore_wait(near_sem, 1)
        for i in range(5):
            x_copy(1, i).start()

    pl.semaphore_wait(barrier, 1 + has_up.astype(jnp.int32) + has_down.astype(jnp.int32))
    pl.semaphore_signal(near_sem, inc=1, device_id=(right, gz), device_id_type=MESH)
    for i in range(5):
        x_copy(0, i).start()

    @pl.when(gx > 0)
    def _():
        towards_left()

    @pl.when(jnp.logical_not(has_down))
    def _():
        def clear(x, carry):
            s0[:, x, :, pl.ds(BASE0 - 1, 1), :] = jnp.zeros((FIELDS, YT, 1, LANES), jnp.float32)
            return carry

        lax.fori_loop(0, CX + 4, clear, 0)

    @pl.when(jnp.logical_not(has_up))
    def _():
        def clear(x, carry):
            s0[:, x, :, pl.ds(BASE0 + CZ, 2), :] = jnp.zeros((FIELDS, YT, 2, LANES), jnp.float32)
            return carry

        lax.fori_loop(0, CX + 4, clear, 0)

        def clear_next(x, carry):
            s1[:, x, :, pl.ds(CZ, 2), :] = jnp.zeros((FIELDS, YT, 2, LANES), jnp.float32)
            cs[:, :, x, :, pl.ds(CZ, 1), :] = jnp.zeros((2, ORDERS, YT, 1, LANES), jnp.float32)
            return carry

        lax.fori_loop(0, CX + 2, clear_next, 0)

    for which in range(2):
        for k in range(YT):
            loads[k][which].wait()

    for group in (3, 0, 1, 2):

        @pl.when(has_up)
        def _(group=group):
            z_copy(group, 0).start()

        @pl.when(has_down)
        def _(group=group):
            z_copy(group, 1).start()

    for k in range(YT):
        loads[k][2].wait()

    def trig(x, carry):
        for k in range(ORDERS):
            for half in range(2):
                store_trig(cs, k, x + 1, pl.ds(8 * half, 8), slice(None), g[k, x, :, pl.ds(8 * half, 8), :])
        return carry

    lax.fori_loop(0, 2, lambda i, carry: trig((CX - 1) * i, carry), 0)

    @pl.when(has_down)
    def _():
        c_copy(0).start()
        c_copy(1).start()

    lax.fori_loop(1, CX - 1, trig, 0)

    @pl.when(has_down)
    def _():
        c_copy(2).start()

    frame_load.wait()
    for step in range(STEPS):
        for half in range(3):
            z = gz * CZ + 8 * half + step + lax.broadcasted_iota(jnp.int32, (1, 8, LANES), 1)
            height = (NZ // 2 - z - frames[step]).astype(jnp.float32)
            heat[step, half] = 2.4 * jnp.tanh(height * 0.125)

    def units_of(group, lower, upper):
        xa = jnp.where(group < 3, 4 + 4 * group, jnp.where(group == 3, 14, CX - 1))
        xb = jnp.where(group < 3, xa + 1, jnp.where(group == 3, 1, 0))
        xc = jnp.where(group < 2, xa + 2, jnp.where(group == 2, 2, xa))
        xd = jnp.where(group < 3, xc + 1, xb)
        return ((xa, lower), (xb, lower), (xc, upper), (xd, upper))

    def arrange(depth):
        def field(f, carry):
            for side in range(2):
                xi = 1 - depth if side == 0 else CX + 2 + depth
                for k in range(YT):
                    s0[f, xi, k, pl.ds(BASE0, CZ), :] = xh[side, depth, f, :, pl.ds(k * LANES, LANES)]
            return carry

        lax.fori_loop(0, FIELDS, field, 0)

    def both(action, which):
        for way in range(2):
            for i in which:
                copy = x_copy(way, i)
                copy.wait_send() if action == "send" else copy.wait_recv()

    def first_step(i, carry):
        group = jnp.where(i < 4, i, jnp.where(i == RIMS_AT, 4, jnp.where(i < RIMS_AT, i - 4, i - 5)))

        @pl.when(jnp.logical_and(has_down, i == 0))
        def _():
            z_copy(1, 0).wait_recv()

        @pl.when(jnp.logical_and(has_down, i == 1))
        def _():
            z_copy(2, 0).wait_recv()

        @pl.when(jnp.logical_and(has_down, i == 2))
        def _():
            z_copy(0, 0).wait_recv()
            z_copy(3, 0).wait_recv()

        @pl.when(i == 3)
        def _():
            @pl.when(has_up)
            def _():
                for every in (3, 0, 1, 2):
                    z_copy(every, 1).wait_recv()

            @pl.when(gx == 0)
            def _():
                towards_left()

            for way in range(2):

                @pl.when(has_up)
                def _(way=way):
                    f_copy(0, way).start()
                    c_copy(1 - way).wait_recv()
                    f_copy(1, way).start()

                @pl.when(has_down)
                def _(way=way):
                    f_copy(2, way).start()

        @pl.when(i == RIMS_AT)
        def _():
            both("recv", (0, 1))
            arrange(0)

        whole = jnp.logical_or(i == 3, i == RIMS_AT)
        units = units_of(group, jnp.where(jnp.logical_or(i < 4, whole), 0, 1), jnp.where(i < 3, 0, 1))
        first_units(s0, s1, cs, heat, units)

        @pl.when(jnp.logical_and(has_down, jnp.logical_or(i < 4, whole)))
        def _():
            m_copy(units[0][0]).start()
            m_copy(units[1][0]).start()

            @pl.when(i < 3)
            def _():
                m_copy(units[2][0]).start()
                m_copy(units[3][0]).start()

        return carry

    lax.fori_loop(0, 8, first_step, 0)

    def second_step(i, carry):
        @pl.when(jnp.logical_and(has_up, i == 3))
        def _():
            c_copy(2).wait_recv()
            for x in range(3, 9):
                m_copy(x).wait_recv()

        @pl.when(jnp.logical_and(has_up, i == 4))
        def _():
            for x in range(9, 13):
                m_copy(x).wait_recv()

        @pl.when(jnp.logical_and(has_up, i == 5))
        def _():
            for x in (13, 14, 1, 2):
                m_copy(x).wait_recv()

        @pl.when(jnp.logical_and(has_up, i == 6))
        def _():
            m_copy(CX - 1).wait_recv()
            m_copy(0).wait_recv()

        group = jnp.where(i < 3, i, i - 3)
        lower = jnp.where(jnp.logical_and(i >= 3, i < 6), 1, 0)
        second_units(o, s1, cs, heat, units_of(group, lower, jnp.where(i < 3, 0, 1)), 0)
        return carry

    lax.fori_loop(0, 7, second_step, 0)
    clear_top(o, has_up)

    both("recv", (2,))

    def outer_trig(k, carry):
        for side in range(2):
            for half in range(2):
                for j in range(YT):
                    part = gh[side, k, pl.ds(8 * half, 8), pl.ds(j * LANES, LANES)]
                    store_trig(cs, k, (CX + 1) * side, pl.ds(8 * half, 8), j, part)
        return carry

    lax.fori_loop(0, ORDERS, outer_trig, 0)
    both("recv", (3, 4))
    arrange(1)

    @pl.when(has_up)
    def _():
        for way in range(2):
            f_copy(0, way).wait_recv()
            f_copy(1, way).wait_recv()

    @pl.when(has_down)
    def _():
        for way in range(2):
            f_copy(2, way).wait_recv()

    def outer_step(t, carry):
        first_units(s0, s1, cs, heat, ((-1, t), (CX, t)))
        return carry

    lax.fori_loop(0, 3, outer_step, 0)

    both("send", range(5))

    @pl.when(has_up)
    def _():
        for group in range(GROUPS):
            z_copy(group, 0).wait_send()
        for way in range(2):
            f_copy(0, way).wait_send()
            f_copy(1, way).wait_send()

    @pl.when(has_down)
    def _():
        for group in range(GROUPS):
            z_copy(group, 1).wait_send()
        for x in range(CX):
            m_copy(x).wait_send()
        for part in range(3):
            c_copy(part).wait_send()
        for way in range(2):
            f_copy(2, way).wait_send()


def finish(o, s1, cs, heat, phase_out, solute_out, rims, sem):
    inner = pl.ds(1, CX - 2)
    copies = [
        pltpu.make_async_copy(o.at[pl.ds(0, ORDERS), inner], phase_out.at[:, inner], sem.at[0]),
        pltpu.make_async_copy(o.at[ORDERS, inner], solute_out.at[inner], sem.at[1]),
    ]
    for copy in copies:
        copy.start()
    for i, x in enumerate((0, CX - 1)):
        second_units(rims.at[:, pl.ds(i, 1)], s1, cs, heat, ((x, 0), (x, 1)), x)
    clear_top(rims, lax.axis_index("gz") < lax.axis_size("gz") - 1)
    for i, x in enumerate((0, CX - 1)):
        ends = [
            pltpu.make_async_copy(rims.at[pl.ds(0, ORDERS), i], phase_out.at[:, x], sem.at[2 + 2 * i]),
            pltpu.make_async_copy(rims.at[ORDERS, i], solute_out.at[x], sem.at[3 + 2 * i]),
        ]
        for copy in ends:
            copy.start()
        copies += ends
    for copy in copies:
        copy.wait()


def local(phase, solute, grain_map, frame_steps):
    hbm, vmem = pl.BlockSpec(memory_space=pltpu.HBM), pl.BlockSpec(memory_space=pltpu.VMEM)
    dma = pltpu.SemaphoreType.DMA
    args = [pltpu.with_memory_space_constraint(a, pltpu.HBM) for a in (frame_steps, phase, solute, grain_map)]
    results = pl.pallas_call(
        kernel,
        out_shape=(
            pltpu.VMEM((FIELDS, CX, CZ, NY), jnp.float32),
            pltpu.VMEM((FIELDS, CX + 2, YT, 24, LANES), jnp.float32),
            pltpu.VMEM((2, ORDERS, CX + 2, YT, 24, LANES), jnp.float32),
            pltpu.VMEM((STEPS, 3, 1, 8, LANES), jnp.float32),
        ),
        in_specs=[hbm] * 4,
        out_specs=(vmem,) * 4,
        scratch_shapes=[
            pltpu.VMEM((FIELDS, CX + 4, YT, 40, LANES), jnp.float32),
            pltpu.VMEM((ORDERS, CX, YT, CZ, LANES), jnp.int32),
            pltpu.VMEM((2, 2, FIELDS, CZ, NY), jnp.float32),
            pltpu.VMEM((2, ORDERS, CZ, NY), jnp.int32),
            pltpu.SMEM((STEPS,), jnp.int32),
            dma((3, YT)),
            dma,
            pltpu.SemaphoreType.REGULAR,
            dma((2, 5)),
            dma((2, 5)),
            dma((2, GROUPS)),
            dma((2, GROUPS)),
            dma((CX,)),
            dma((CX,)),
            dma((3,)),
            dma((3,)),
            dma((3, 2)),
            dma((3, 2)),
        ],
        compiler_params=pltpu.CompilerParams(
            collective_id=0, has_side_effects=True, vmem_limit_bytes=32 * 1024 * 1024
        ),
        name="grow",
    )(*args)
    return pl.pallas_call(
        finish,
        out_shape=(
            pltpu.HBM(phase.shape, jnp.float32),
            pltpu.HBM(solute.shape, jnp.float32),
        ),
        in_specs=[vmem] * 4,
        out_specs=(hbm, hbm),
        scratch_shapes=[pltpu.VMEM((FIELDS, 2, CZ, NY), jnp.float32), dma((6,))],
        compiler_params=pltpu.CompilerParams(vmem_limit_bytes=16 * 1024 * 1024),
        name="finish",
    )(*results)


def solution(mesh):
    in_specs = (P(None, "gx", "gz", None), P("gx", "gz", None), P(None, "gx", "gz", None), P())
    out_specs = (P(None, "gx", "gz", None), P("gx", "gz", None))
    return jax.shard_map(local, mesh=mesh, in_specs=in_specs, out_specs=out_specs, check_vma=False)
```

time: 23 us -> 24.9 us (1.083)
  the two profiles are of different devices: /device:TPU:97 before, /device:TPU:31 now
where the time goes in v7:
time: 24.9 us; the launch traced here: 24.8 us
  Pallas kernels  24.2 us (97%)
  between operations  0.64 us (3%)
    pallas_call x1, Pallas kernels, local(): pl.pallas_call(kernel, out_shape=(pltpu.VMEM((FIELDS, CX, CZ, NY), jnp.fl...  22.4 us
    pallas_call x1, Pallas kernels, local(): pl.pallas_call(finish, out_shape=(pltpu.HBM(phase.shape, jnp.float32), pl...  1.74 us

profile of v7, /device:TPU:31, one launch (start us, length us, event | category | flops | bytes accessed | tf_op | source)
XLA Modules:
  0.0 24.8 jit_solution(6587446307814038924)
XLA Ops:
  0.6 22.4 %grow.1 = (f32[5,16,16,512]{3,2,1,0:T(8,128)S(1)}, f32[5,18,4,24,128]{4,3,2,1,0:T(8,128)S(1)}, f32[2,4,18,4,24,128]{5,4,3,2,1,0:T(8,128)S(1)}, f32[2,3,1,8,128]{4,3,2,1,0:T(8,128)S(1)}) custom-call(s32[2]{0:T(128)} %frames_in.1, f32[4,16,16,512]{3,2,1,0:T(8,128)} %phase.1, f32[16,16,512]{2,1,0:T(8,128)} %solute.1, s32[4,16,16,512]{3,2,1,0:T(8,128)} %grain.1), custom_call_target="tpu_custom_call" | custom-call | tf_op jit(solution)/shard_map/grow/pallas_call | solution.py:528
  23.1 1.7 %finish.1 = (f32[4,16,16,512]{3,2,1,0:T(8,128)}, f32[16,16,512]{2,1,0:T(8,128)}) custom-call(f32[5,16,16,512]{3,2,1,0:T(8,128)S(1)} %get-tuple-element.6.o, f32[5,18,4,24,128]{4,3,2,1,0:T(8,128)S(1)} %get-tuple-element.7.s1, f32[2,4,18,4,24,128]{5,4,3,2,1,0:T(8,128)S(1)} %get-tuple-element.8.cs, f32[2,3,1,8,128]{4,3,2,1,0:T(8,128)S(1)} %get-tuple-element.9.heat), custom_call_target="tpu_custom_call" | custom-call | tf_op jit(solution)/shard_map/finish/pallas_call | solution.py:563

commit v8 on v6

--- a/solution.py
+++ b/solution.py
@@ -24,7 +24,9 @@
 
 BASE0 = 8
 
-RIMS_AT = 5
+ABOVE = BASE0 + CZ + 2
+
+RIMS_AT = 0
 
 
 def sine_coefficients():
@@ -55,22 +57,19 @@
     return jnp.concatenate([rolled[-1:], rolled[:-1]], axis=0)
 
 
-def neighbours(s, f, xi, row, part):
-    at = pl.ds(row, 8)
+def neighbours(load, f, part):
     ys = slice(None) if part is None else pl.ds(2 * part, 2)
-    c = s[f, xi, ys, at, :]
-    xl = s[f, xi - 1, ys, at, :]
-    xh = s[f, xi + 1, ys, at, :]
-    zl = s[f, xi, ys, pl.ds(row - 1, 8), :]
-    zh = s[f, xi, ys, pl.ds(row + 1, 8), :]
+    c = load(f, 0, 0, ys)
+    xl, xh = load(f, -1, 0, ys), load(f, 1, 0, ys)
+    zl, zh = load(f, 0, -1, ys), load(f, 0, 1, ys)
     lane = lax.broadcasted_iota(jnp.int32, c.shape, 2)
     right = pltpu.roll(c, 1, axis=2)
     left = pltpu.roll(c, LANES - 1, axis=2)
     if part is None:
         before, after = next_y(right, -1), next_y(left, 1)
     else:
-        before = s[f, xi, pl.ds(lax.rem(2 * part + YT - 1, YT), 1), at, :]
-        after = s[f, xi, pl.ds(lax.rem(2 * part + 2, YT), 1), at, :]
+        before = load(f, 0, 0, pl.ds(lax.rem(2 * part + YT - 1, YT), 1))
+        after = load(f, 0, 0, pl.ds(lax.rem(2 * part + 2, YT), 1))
         before = jnp.concatenate([pltpu.roll(before, 1, axis=2), right[:1]], axis=0)
         after = jnp.concatenate([left[1:], pltpu.roll(after, LANES - 1, axis=2)], axis=0)
     yl = jnp.where(lane == 0, before, right)
@@ -78,25 +77,22 @@
     return c, xl, xh, yl, yh, zl, zh
 
 
-def advance(s, cs, x, row, cs_row, thermal, put, part=None):
-    xi = x + 1
+def advance(load, table, thermal, put, part=None):
     ys = slice(None) if part is None else pl.ds(2 * part, 2)
-    u = s[ORDERS, xi, ys, pl.ds(row, 8), :]
-    drive = thermal - 2.4 * u
+    drive = thermal - 2.4 * load(ORDERS, 0, 0, ys)
     q = None
     for k in range(ORDERS):
-        p = s[k, xi, ys, pl.ds(row, 8), :]
+        p = load(k, 0, 0, ys)
         q = p * p if q is None else q + p * p
     well = 0.64 - 0.16 * q
     total = None
     for k in range(ORDERS):
-        p, xl, xh, yl, yh, zl, zh = neighbours(s, k, xi, row, part)
+        p, xl, xh, yl, yh, zl, zh = neighbours(load, k, part)
         gx, gy, gz = xh - xl, yh - yl, zh - zl
         lap = (xl + xh) + (yl + yh) + (zl + zh) - 6.0 * p
         x2, y2, z2 = gx * gx, gy * gy, gz * gz
         r = x2 + y2
-        at = pl.ds(cs_row, 8)
-        t = cs[0, k, x, ys, at, :] * (gx * gy) + cs[1, k, x, ys, at, :] * (x2 - y2)
+        t = table(0, k, ys) * (gx * gy) + table(1, k, ys) * (x2 - y2)
         quartic = r * r + z2 * z2 - t * t
         d = (r + z2) + 0.2
         ratio = quartic * pl.reciprocal(d * d, approx=True)
@@ -108,9 +104,53 @@
         )
         put(k, p + delta)
         total = delta if total is None else total + delta
-    c, xl, xh, yl, yh, zl, zh = neighbours(s, ORDERS, xi, row, part)
+    c, xl, xh, yl, yh, zl, zh = neighbours(load, ORDERS, part)
     near = (xl + xh) + (yl + yh) + (zl + zh)
     put(ORDERS, 0.52 * c + 0.08 * near + 0.5 * total)
+
+
+def advance_tile(s, cs, x, row, cs_row, thermal, put, part=None):
+    def load(f, dx, dz, ys):
+        return s[f, x + 1 + dx, ys, pl.ds(row + dz, 8), :]
+
+    def table(i, k, ys):
+        return cs[i, k, x, ys, pl.ds(cs_row, 8), :]
+
+    advance(load, table, thermal, put, part)
+
+
+def advance_row(s, s_new, cs, x, row, above, z, thermal):
+    def load(f, dx, dz, ys):
+        flat, rows = strided(s, f, x + 1 + dx, above if dz > 0 else row + dz)
+        return jnp.stack([flat[r, :] for r in rows])
+
+    def table(i, k, ys):
+        flat, rows = strided(cs, i, k, x, z)
+        return jnp.stack([flat[r, :] for r in rows])
+
+    def put(f, value):
+        flat, rows = strided(s_new, f, x + 1, z)
+        for k in range(YT):
+            flat[rows[k], :] = value[k]
+
+    advance(load, table, thermal, put)
+
+
+def sine_cosine(grain):
+    h = ((grain & 255) - 128).astype(jnp.float32)
+    h2 = h * h
+    return h * horner(h2, SIN_C), horner(h2, COS_C)
+
+
+def strided(ref, *at):
+    *outer, plane, where = at
+    planes, rows = ref.shape[-4], ref.shape[-2]
+    first = 0
+    for size, index in zip(ref.shape, outer):
+        first = first * size + index
+    first = (first * planes + plane) * YT * rows + where
+    flat = ref.reshape(math.prod(ref.shape[:-1]), LANES)
+    return flat, [pl.ds(first + k * rows, 8, stride=YT * rows) for k in range(YT)]
 
 
 def tile(half):
@@ -124,7 +164,7 @@
             for k in range(YT):
                 o[f, x - first, tile(half), pl.ds(k * LANES, LANES)] = value[k]
 
-        advance(s1, cs, x, 1 + 8 * half, 1 + 8 * half, heat[1, half], put)
+        advance_tile(s1, cs, x, 1 + 8 * half, 1 + 8 * half, heat[1, half], put)
 
 
 def clear_top(o, has_up):
@@ -139,7 +179,7 @@
 
 def kernel(
     frames_in, phase, solute, grain, o, s1, cs, heat,
-    s0, g, frames,
+    s0, g, low, frames,
     load_sem, frame_sem, x_send, x_recv, z_send, z_recv, m_send, m_recv, c_send, c_recv, d_send, d_recv,
 ):
     gx, gz = lax.axis_index("gx"), lax.axis_index("gz")
@@ -196,7 +236,7 @@
     @pl.when(jnp.logical_not(has_up))
     def _():
         def clear(x, carry):
-            s0[:, x, :, pl.ds(BASE0 + CZ, 1), :] = jnp.zeros((FIELDS, YT, 1, LANES), jnp.float32)
+            s0[:, x, :, pl.ds(ABOVE, 1), :] = jnp.zeros((FIELDS, YT, 1, LANES), jnp.float32)
             s1[:, x, :, pl.ds(CZ, 2), :] = jnp.zeros((FIELDS, YT, 2, LANES), jnp.float32)
             return carry
 
@@ -229,7 +269,7 @@
 
     def z_copy(group, way):
         planes = pl.ds(1 + group * GROUP, GROUP)
-        src, dst, to = (BASE0 + CZ - 1, BASE0 - 1, gz + 1) if way == 0 else (BASE0, BASE0 + CZ, gz - 1)
+        src, dst, to = (BASE0 + CZ - 1, BASE0 - 1, gz + 1) if way == 0 else (BASE0, ABOVE, gz - 1)
         return remote(
             s0.at[:, planes, :, pl.ds(src, 1), :],
             s0.at[:, planes, :, pl.ds(dst, 1), :],
@@ -261,9 +301,7 @@
         )
 
     def c_copy():
-        return remote(
-            cs.at[:, :, :, :, pl.ds(0, 1), :], cs.at[:, :, :, :, pl.ds(CZ, 1), :], c_send, c_recv, gx, gz - 1
-        )
+        return remote(grain.at[:, :, 0, :], low, c_send, c_recv, gx, gz - 1)
 
     for which in range(2):
         for k in range(YT):
@@ -284,6 +322,10 @@
         def _(group=group):
             z_copy(group, 1).start()
 
+    @pl.when(has_down)
+    def _():
+        c_copy().start()
+
     for k in range(YT):
         loads[k][2].wait()
 
@@ -291,17 +333,10 @@
         for k in range(ORDERS):
             for half in range(2):
                 at = pl.ds(8 * half, 8)
-                h = ((g[k, x, :, at, :] & 255) - 128).astype(jnp.float32)
-                h2 = h * h
-                cs[0, k, x, :, at, :] = h * horner(h2, SIN_C)
-                cs[1, k, x, :, at, :] = horner(h2, COS_C)
+                cs[0, k, x, :, at, :], cs[1, k, x, :, at, :] = sine_cosine(g[k, x, :, at, :])
         return carry
 
     lax.fori_loop(0, CX, trig, 0)
-
-    @pl.when(has_down)
-    def _():
-        c_copy().start()
 
     frame_load.wait()
     for step in range(STEPS):
@@ -316,7 +351,7 @@
             def put(f, value, x=x, half=half):
                 s1[f, x + 1, :, tile(half), :] = value
 
-            advance(s0, cs, x, BASE0 + 8 * half, 8 * half, heat[0, half], put)
+            advance_tile(s0, cs, x, BASE0 + 8 * half, 8 * half, heat[0, half], put)
 
     def units_of(group, lower, upper):
         xa = jnp.where(group < 3, 4 + 4 * group, 14)
@@ -327,6 +362,16 @@
 
     def first_rims(piece, carry):
         half, part = lax.div(piece, 2), lax.rem(piece, 2)
+        @pl.when(piece == 2)
+        def _():
+            @pl.when(has_up)
+            def _():
+                z_copy(0, 1).wait_recv()
+                z_copy(3, 1).wait_recv()
+
+            for xi in (1, CX):
+                s0[:, xi, :, pl.ds(BASE0 + CZ, 1), :] = s0[:, xi, :, pl.ds(ABOVE, 1), :]
+
         x_copy(0, 0, piece).wait_recv()
         x_copy(0, 1, piece).wait_recv()
         for x in (CX - 1, 0):
@@ -334,7 +379,7 @@
             def put(f, value, x=x):
                 s1[f, x + 1, pl.ds(2 * part, 2), tile(half), :] = value
 
-            advance(s0, cs, x, BASE0 + 8 * half, 8 * half, heat[0, half], put, part)
+            advance_tile(s0, cs, x, BASE0 + 8 * half, 8 * half, heat[0, half], put, part)
         x_copy(1, 0, piece).start()
         x_copy(1, 1, piece).start()
 
@@ -356,15 +401,6 @@
         @pl.when(jnp.logical_and(has_down, i == 2))
         def _():
             z_copy(0, 0).wait_recv()
-
-        @pl.when(jnp.logical_and(has_up, i == 3))
-        def _():
-            for every in (1, 2, 3, 0):
-                z_copy(every, 1).wait_recv()
-
-        @pl.when(i == RIMS_AT)
-        def _():
-            lax.fori_loop(0, 4, first_rims, 0)
 
         units = units_of(group, lax.div(i, 4), jnp.where(i < 3, 0, 1))
         first_units(units)
@@ -384,9 +420,38 @@
     lax.fori_loop(0, 7, first_step, 0)
 
     def second_step(i, carry):
+        @pl.when(i == RIMS_AT)
+        def _():
+            lax.fori_loop(0, 4, first_rims, 0)
+
+        @pl.when(i == 3)
+        def _():
+            @pl.when(has_up)
+            def _():
+                z_copy(1, 1).wait_recv()
+                z_copy(2, 1).wait_recv()
+
+            def top(j, carry):
+                row = jnp.broadcast_to(heat[0, 1, :, pl.ds(7, 1), :], (1, 8, LANES))
+                advance_row(s0, s1, cs, 1 + 6 * j, BASE0 + CZ - 1, ABOVE, CZ - 1, row)
+                return carry
+
+            lax.fori_loop(0, 2, top, 0)
+
         @pl.when(jnp.logical_and(has_up, i == 3))
         def _():
             c_copy().wait_recv()
+
+            def above_trig(k, carry):
+                for x in (0, 8):
+                    for i in range(2):
+                        flat, rows = strided(cs, i, k, x, CZ)
+                        for j in range(YT):
+                            part = low[k, pl.ds(x, 8), pl.ds(j * LANES, LANES)]
+                            flat[rows[j], :] = sine_cosine(part)[i]
+                return carry
+
+            lax.fori_loop(0, ORDERS, above_trig, 0)
             for x in range(3, 9):
                 m_copy(x).wait_recv()
 
@@ -481,6 +546,7 @@
         scratch_shapes=[
             pltpu.VMEM((FIELDS, CX + 2, YT, 32, LANES), jnp.float32),
             pltpu.VMEM((ORDERS, CX, YT, CZ, LANES), jnp.int32),
+            pltpu.VMEM((ORDERS, CX, NY), jnp.int32),
             pltpu.SMEM((STEPS,), jnp.int32),
             dma((3, YT)),
             dma,

time: 23 us -> 22.1 us (0.961)
  Pallas kernels: 22.3 us -> 21.4 us
    pallas_call x1, Pallas kernels: 20.6 us -> 19.7 us  [local(): pl.pallas_call(kernel, out_shape=(pltpu.VMEM((FIELDS, CX, CZ, NY), jnp.fl...]
where the time goes in v8:
time: 22.1 us
  Pallas kernels  21.4 us (97%)
  between operations  0.64 us (3%)
    pallas_call x1, Pallas kernels, local(): pl.pallas_call(kernel, out_shape=(pltpu.VMEM((FIELDS, CX, CZ, NY), jnp.fl...  19.7 us
    pallas_call x1, Pallas kernels, local(): pl.pallas_call(finish, out_shape=(pltpu.HBM(phase.shape, jnp.float32), pl...  1.74 us

profile of v8, /device:TPU:97, one launch (start us, length us, event | category | flops | bytes accessed | tf_op | source)
XLA Modules:
  0.0 22.1 jit_solution(11304870262263232755)
XLA Ops:
  0.6 19.7 %grow.1 = (f32[5,16,16,512]{3,2,1,0:T(8,128)S(1)}, f32[5,18,4,24,128]{4,3,2,1,0:T(8,128)S(1)}, f32[2,4,16,4,24,128]{5,4,3,2,1,0:T(8,128)S(1)}, f32[2,2,1,8,128]{4,3,2,1,0:T(8,128)S(1)}) custom-call(s32[2]{0:T(128)} %frames_in.1, f32[4,16,16,512]{3,2,1,0:T(8,128)} %phase.1, f32[16,16,512]{2,1,0:T(8,128)} %solute.1, s32[4,16,16,512]{3,2,1,0:T(8,128)} %grain.1), custom_call_target="tpu_custom_call" | custom-call | tf_op jit(solution)/shard_map/grow/pallas_call | solution.py:536
  20.3 1.7 %finish.1 = (f32[4,16,16,512]{3,2,1,0:T(8,128)}, f32[16,16,512]{2,1,0:T(8,128)}) custom-call(f32[5,16,16,512]{3,2,1,0:T(8,128)S(1)} %get-tuple-element.6.o, f32[5,18,4,24,128]{4,3,2,1,0:T(8,128)S(1)} %get-tuple-element.7.s1, f32[2,4,16,4,24,128]{5,4,3,2,1,0:T(8,128)S(1)} %get-tuple-element.8.cs, f32[2,2,1,8,128]{4,3,2,1,0:T(8,128)S(1)} %get-tuple-element.9.heat), custom_call_target="tpu_custom_call" | custom-call | tf_op jit(solution)/shard_map/finish/pallas_call | solution.py:569

commit v9 on v8

--- a/solution.py
+++ b/solution.py
@@ -312,15 +312,15 @@
     for piece in range(4):
         x_copy(0, 0, piece).start()
         x_copy(0, 1, piece).start()
-    for group in (1, 2, 3, 0):
-
-        @pl.when(has_up)
-        def _(group=group):
+    @pl.when(has_down)
+    def _():
+        for group in (3, 0, 1, 2):
+            z_copy(group, 1).start()
+
+    @pl.when(has_up)
+    def _():
+        for group in (1, 2, 3, 0):
             z_copy(group, 0).start()
-
-        @pl.when(has_down)
-        def _(group=group):
-            z_copy(group, 1).start()
 
     @pl.when(has_down)
     def _():
@@ -385,9 +385,10 @@
 
         @pl.when(jnp.logical_and(piece == 1, has_down))
         def _():
-            for way, x in ((0, CX - 1), (1, 0)):
-                m_copy(x).start()
+            for way in range(2):
                 d_copy(way).start()
+            m_copy(CX - 1).start()
+            m_copy(0).start()
 
         return carry
 

time: 22.1 us -> 21.9 us (level)
  no operation moved by 1% of the time
where the time goes in v9:
time: 21.9 us; the launch traced here: 21.8 us
  Pallas kernels  21.2 us (97%)
  between operations  0.64 us (3%)
    pallas_call x1, Pallas kernels, local(): pl.pallas_call(kernel, out_shape=(pltpu.VMEM((FIELDS, CX, CZ, NY), jnp.fl...  19.5 us
    pallas_call x1, Pallas kernels, local(): pl.pallas_call(finish, out_shape=(pltpu.HBM(phase.shape, jnp.float32), pl...  1.74 us

profile of v9, /device:TPU:97, one launch (start us, length us, event | category | flops | bytes accessed | tf_op | source)
XLA Modules:
  0.0 21.8 jit_solution(11307546955991434937)
XLA Ops:
  0.6 19.5 %grow.1 = (f32[5,16,16,512]{3,2,1,0:T(8,128)S(1)}, f32[5,18,4,24,128]{4,3,2,1,0:T(8,128)S(1)}, f32[2,4,16,4,24,128]{5,4,3,2,1,0:T(8,128)S(1)}, f32[2,2,1,8,128]{4,3,2,1,0:T(8,128)S(1)}) custom-call(s32[2]{0:T(128)} %frames_in.1, f32[4,16,16,512]{3,2,1,0:T(8,128)} %phase.1, f32[16,16,512]{2,1,0:T(8,128)} %solute.1, s32[4,16,16,512]{3,2,1,0:T(8,128)} %grain.1), custom_call_target="tpu_custom_call" | custom-call | tf_op jit(solution)/shard_map/grow/pallas_call | solution.py:537
  20.1 1.7 %finish.1 = (f32[4,16,16,512]{3,2,1,0:T(8,128)}, f32[16,16,512]{2,1,0:T(8,128)}) custom-call(f32[5,16,16,512]{3,2,1,0:T(8,128)S(1)} %get-tuple-element.6.o, f32[5,18,4,24,128]{4,3,2,1,0:T(8,128)S(1)} %get-tuple-element.7.s1, f32[2,4,16,4,24,128]{5,4,3,2,1,0:T(8,128)S(1)} %get-tuple-element.8.cs, f32[2,2,1,8,128]{4,3,2,1,0:T(8,128)S(1)} %get-tuple-element.9.heat), custom_call_target="tpu_custom_call" | custom-call | tf_op jit(solution)/shard_map/finish/pallas_call | solution.py:570

commit v10 on v9

--- a/solution.py
+++ b/solution.py
@@ -515,10 +515,11 @@
     ]
     for copy in copies:
         copy.start()
+    has_up = lax.axis_index("gz") < lax.axis_size("gz") - 1
     for i, x in enumerate((0, CX - 1)):
-        second_units(rims.at[:, pl.ds(i, 1)], s1, cs, heat, ((x, 0), (x, 1)), x)
-    clear_top(rims, lax.axis_index("gz") < lax.axis_size("gz") - 1)
-    for i, x in enumerate((0, CX - 1)):
+        rim = rims.at[:, pl.ds(i, 1)]
+        second_units(rim, s1, cs, heat, ((x, 0), (x, 1)), x)
+        clear_top(rim, has_up)
         ends = [
             pltpu.make_async_copy(rims.at[pl.ds(0, ORDERS), i], phase_out.at[:, x], sem.at[2 + 2 * i]),
             pltpu.make_async_copy(rims.at[ORDERS, i], solute_out.at[x], sem.at[3 + 2 * i]),

time: 21.9 us -> 21.7 us (level)
  no operation moved by 1% of the time
where the time goes in v10:
time: 21.7 us; the launch traced here: 21.6 us
  Pallas kernels  21 us (97%)
  between operations  0.64 us (3%)
    pallas_call x1, Pallas kernels, local(): pl.pallas_call(kernel, out_shape=(pltpu.VMEM((FIELDS, CX, CZ, NY), jnp.fl...  19.5 us
    pallas_call x1, Pallas kernels, local(): pl.pallas_call(finish, out_shape=(pltpu.HBM(phase.shape, jnp.float32), pl...  1.53 us

profile of v10, /device:TPU:97, one launch (start us, length us, event | category | flops | bytes accessed | tf_op | source)
XLA Modules:
  0.0 21.6 jit_solution(7227261980395788559)
XLA Ops:
  0.6 19.5 %grow.1 = (f32[5,16,16,512]{3,2,1,0:T(8,128)S(1)}, f32[5,18,4,24,128]{4,3,2,1,0:T(8,128)S(1)}, f32[2,4,16,4,24,128]{5,4,3,2,1,0:T(8,128)S(1)}, f32[2,2,1,8,128]{4,3,2,1,0:T(8,128)S(1)}) custom-call(s32[2]{0:T(128)} %frames_in.1, f32[4,16,16,512]{3,2,1,0:T(8,128)} %phase.1, f32[16,16,512]{2,1,0:T(8,128)} %solute.1, s32[4,16,16,512]{3,2,1,0:T(8,128)} %grain.1), custom_call_target="tpu_custom_call" | custom-call | tf_op jit(solution)/shard_map/grow/pallas_call | solution.py:538
  20.1 1.5 %finish.1 = (f32[4,16,16,512]{3,2,1,0:T(8,128)}, f32[16,16,512]{2,1,0:T(8,128)}) custom-call(f32[5,16,16,512]{3,2,1,0:T(8,128)S(1)} %get-tuple-element.6.o, f32[5,18,4,24,128]{4,3,2,1,0:T(8,128)S(1)} %get-tuple-element.7.s1, f32[2,4,16,4,24,128]{5,4,3,2,1,0:T(8,128)S(1)} %get-tuple-element.8.cs, f32[2,2,1,8,128]{4,3,2,1,0:T(8,128)S(1)} %get-tuple-element.9.heat), custom_call_target="tpu_custom_call" | custom-call | tf_op jit(solution)/shard_map/finish/pallas_call | solution.py:571

commit v11 on v10

--- a/solution.py
+++ b/solution.py
@@ -374,14 +374,13 @@
 
         x_copy(0, 0, piece).wait_recv()
         x_copy(0, 1, piece).wait_recv()
-        for x in (CX - 1, 0):
+        for way, x in ((0, CX - 1), (1, 0)):
 
             def put(f, value, x=x):
                 s1[f, x + 1, pl.ds(2 * part, 2), tile(half), :] = value
 
             advance_tile(s0, cs, x, BASE0 + 8 * half, 8 * half, heat[0, half], put, part)
-        x_copy(1, 0, piece).start()
-        x_copy(1, 1, piece).start()
+            x_copy(1, way, piece).start()
 
         @pl.when(jnp.logical_and(piece == 1, has_down))
         def _():

time: 21.7 us -> 21.9 us (level)
  no operation moved by 1% of the time
where the time goes in v11:
time: 21.9 us; the launch traced here: 21.8 us
  Pallas kernels  21.2 us (97%)
  between operations  0.64 us (3%)
    pallas_call x1, Pallas kernels, local(): pl.pallas_call(kernel, out_shape=(pltpu.VMEM((FIELDS, CX, CZ, NY), jnp.fl...  19.6 us
    pallas_call x1, Pallas kernels, local(): pl.pallas_call(finish, out_shape=(pltpu.HBM(phase.shape, jnp.float32), pl...  1.53 us

profile of v11, /device:TPU:97, one launch (start us, length us, event | category | flops | bytes accessed | tf_op | source)
XLA Modules:
  0.0 21.8 jit_solution(943149869123234919)
XLA Ops:
  0.6 19.6 %grow.1 = (f32[5,16,16,512]{3,2,1,0:T(8,128)S(1)}, f32[5,18,4,24,128]{4,3,2,1,0:T(8,128)S(1)}, f32[2,4,16,4,24,128]{5,4,3,2,1,0:T(8,128)S(1)}, f32[2,2,1,8,128]{4,3,2,1,0:T(8,128)S(1)}) custom-call(s32[2]{0:T(128)} %frames_in.1, f32[4,16,16,512]{3,2,1,0:T(8,128)} %phase.1, f32[16,16,512]{2,1,0:T(8,128)} %solute.1, s32[4,16,16,512]{3,2,1,0:T(8,128)} %grain.1), custom_call_target="tpu_custom_call" | custom-call | tf_op jit(solution)/shard_map/grow/pallas_call | solution.py:537
  20.3 1.5 %finish.1 = (f32[4,16,16,512]{3,2,1,0:T(8,128)}, f32[16,16,512]{2,1,0:T(8,128)}) custom-call(f32[5,16,16,512]{3,2,1,0:T(8,128)S(1)} %get-tuple-element.6.o, f32[5,18,4,24,128]{4,3,2,1,0:T(8,128)S(1)} %get-tuple-element.7.s1, f32[2,4,16,4,24,128]{5,4,3,2,1,0:T(8,128)S(1)} %get-tuple-element.8.cs, f32[2,2,1,8,128]{4,3,2,1,0:T(8,128)S(1)} %get-tuple-element.9.heat), custom_call_target="tpu_custom_call" | custom-call | tf_op jit(solution)/shard_map/finish/pallas_call | solution.py:570
